TPU v7x, 128 devices: a whole 4x4x4 slice. The times are simulated.
128 devices in a mesh: seq: 16 (over x, z), tp: 8 (over y, core).
Axes of the slice: x: 4, y: 4, z: 4, core: 2. Of those that a mesh axis runs over, the one named last changes fastest.
Arguments:
- tokens: bfloat16 [8192, 2880], P(('seq', 'tp')), may hold values from -6 to 6
- attn_gain: float32 [2880], replicated, may hold values from 0.1 to 1.9
- moe_gain: float32 [2880], replicated, may hold values from 0.1 to 1.9
- q_weight: bfloat16 [2880, 8, 512], P('seq', 'tp'), may hold values from -0.109375 to 0.109375
- kv_weight: bfloat16 [2880, 8, 128], P('seq', 'tp'), may hold values from -0.109375 to 0.109375
- o_weight: bfloat16 [512, 8, 2880], P('seq', 'tp'), may hold values from -0.75 to 0.75
- sinks: float32 [8, 8], P('tp'), may hold values from 0 to 6
- gate_up: bfloat16 [128, 2880, 2880], P(('seq', 'tp')), may hold values from -0.109375 to 0.109375
- down: bfloat16 [128, 1440, 2880], P(('seq', 'tp')), may hold values from -0.15625 to 0.15625
- expert_ids: int32 [8192, 4], P(('seq', 'tp')), may hold values from 0 to 127, all different within a row; in each aligned block of 64 rows (0 to 63, 64 to 127, ...) at most 4 rows name the same one
- route_weights: float32 [8192, 4], P(('seq', 'tp')), may hold values from 0.05 to 0.6
Outputs:
- attended: bfloat16 [8192, 2880], P(('seq', 'tp'))
- experts_out: bfloat16 [8192, 2880], P(('seq', 'tp'))
Inputs may be any that keep to these rules, and one draw needn't show every extreme that they name: `expert_ids`: A row names 4 different experts. Among the rows of one device (aligned blocks of 64 rows) no expert is named by more than 4 rows, and in every draw some block has an expert named by exactly 4 rows.
All inputs are finite; a program needn't handle non-finite values.
Results may differ from a plain program's by a relative error of at most 0.03.
Values may be sent and summed in bfloat16 or wider, within the bound.
No kernel may reach another device: no remote copies, remote signals or barrier semaphores. Data moves between devices by JAX's collectives and lax.ppermute only.
A program may use at most 128 MiB of HBM per device.

v0:
```python
import jax
import jax.numpy as jnp
from jax import lax
from jax.sharding import PartitionSpec as P

WINDOW = 128


ROPE_BASE = 150000.0


def passed_along(block, axis, distance):
    devices = range(lax.axis_size(axis))
    route = [(i - distance, i) for i in devices if i - distance in devices]
    return lax.ppermute(block, axis, route)


def rms_norm(values, gain):
    wide = values.astype(jnp.float32)
    scale = lax.rsqrt(jnp.mean(wide * wide, axis=-1, keepdims=True) + 1e-05)
    return (wide * scale * gain).astype(jnp.bfloat16)


def rotate(values, positions):
    half = values.shape[-1] // 2
    freq = ROPE_BASE ** (-(jnp.arange(half, dtype=jnp.float32) * 2.0) / (2.0 * half))
    angle = positions * freq
    cosine = jnp.cos(angle)
    sine = jnp.sin(angle)
    first = values[..., :half]
    second = values[..., half:]
    return jnp.concatenate(
        [first * cosine - second * sine, second * cosine + first * sine], axis=-1
    )


def window_attention(query, keys, values, q_pos, k_pos, sinks, window):
    diff = q_pos[:, None] - k_pos[None, :]
    allowed = (diff >= 0) & (diff < window) & (k_pos[None, :] >= 0)
    scale = query.shape[-1] ** (-0.5)
    scores = jnp.einsum("tjgd,sjd->jgts", query, keys, preferred_element_type=jnp.float32) * scale
    expo = jnp.where(allowed[None, None], jnp.exp(scores), 0.0)
    denom = jnp.sum(expo, axis=-1, keepdims=True) + jnp.exp(sinks)[:, :, None, None]
    probs = (expo / denom).astype(jnp.bfloat16)
    out = jnp.einsum("jgts,sjd->tjgd", probs, values, preferred_element_type=jnp.float32)
    return out.astype(jnp.bfloat16).reshape(out.shape[0], out.shape[1], -1)


def expert_ffn(rows, gate_up, down):
    width = down.shape[0]
    both = jnp.dot(rows, gate_up, preferred_element_type=jnp.float32)
    gate = both[:, :width]
    upper = both[:, width:]
    act = ((upper + 1.0) * gate * jax.nn.sigmoid(1.702 * gate)).astype(jnp.bfloat16)
    return jnp.dot(act, down, preferred_element_type=jnp.float32).astype(jnp.bfloat16)


def on_device(
    tokens,
    attn_gain,
    moe_gain,
    q_weight,
    kv_weight,
    o_weight,
    sinks,
    gate_up,
    down,
    expert_ids,
    route_weights,
):
    rows = tokens.shape[0]
    width = tokens.shape[1]
    x_block = lax.all_gather(tokens, "tp", axis=0, tiled=True)
    span = x_block.shape[0]
    normed = rms_norm(x_block, attn_gain)
    q_full, kv_full, o_full = (
        lax.all_gather(q_weight, "seq", axis=0, tiled=True),
        lax.all_gather(kv_weight, "seq", axis=0, tiled=True),
        lax.all_gather(o_weight, "seq", axis=0, tiled=True),
    )
    query = jnp.einsum("td,dhe->the", normed, q_full, preferred_element_type=jnp.float32)
    keyval = jnp.einsum("td,dhe->the", normed, kv_full, preferred_element_type=jnp.float32)
    heads = query.shape[1]
    head_dim = keyval.shape[2] // 2
    group = query.shape[2] // head_dim
    first = lax.axis_index("seq") * span
    positions = first + jnp.arange(span, dtype=jnp.int32)
    pos_float = positions.astype(jnp.float32)
    rq = rotate(query.reshape(span, heads, group, head_dim), pos_float[:, None, None, None]).astype(
        jnp.bfloat16
    )
    rk = rotate(keyval[..., :head_dim], pos_float[:, None, None]).astype(jnp.bfloat16)
    values = keyval[..., head_dim:].astype(jnp.bfloat16)
    tail = jnp.concatenate([rk[span - WINDOW :], values[span - WINDOW :]], axis=2)
    earlier = passed_along(tail, "seq", 1)
    all_keys = jnp.concatenate([earlier[..., :head_dim], rk], axis=0)
    all_values = jnp.concatenate([earlier[..., head_dim:], values], axis=0)
    k_pos = first - WINDOW + jnp.arange(span + WINDOW, dtype=jnp.int32)
    heads_out = window_attention(rq, all_keys, all_values, positions, k_pos, sinks, WINDOW)
    partial_value = jnp.einsum("tjg,gjd->td", heads_out, o_full, preferred_element_type=jnp.float32)
    total = lax.psum(partial_value.astype(jnp.bfloat16), "tp").astype(jnp.float32)
    share = lax.dynamic_slice_in_dim(total, lax.axis_index("tp") * rows, rows, 0)
    attended = (tokens.astype(jnp.float32) + share).astype(jnp.bfloat16)
    moe_in = rms_norm(attended, moe_gain)
    experts = lax.axis_size("seq") * lax.axis_size("tp")
    topk = expert_ids.shape[1]
    slots_each = max(2, 2 * rows * topk // experts)
    picks = expert_ids.reshape(-1)
    count = picks.shape[0]
    onehot = (picks[:, None] == jnp.arange(experts, dtype=jnp.int32)[None, :]).astype(jnp.float32)
    lower = (jnp.arange(count)[:, None] > jnp.arange(count)[None, :]).astype(jnp.float32)
    before = jnp.dot(lower, onehot, precision=lax.Precision.HIGHEST)
    ranks = jnp.arange(slots_each, dtype=jnp.float32)
    slot_hot = onehot[:, :, None] * (before[:, :, None] == ranks[None, None, :]).astype(jnp.float32)
    slot_hot = slot_hot.reshape(rows, topk, experts * slots_each)
    place = jnp.sum(slot_hot, axis=1).astype(jnp.bfloat16)
    weighted = jnp.sum(slot_hot * route_weights[:, :, None], axis=1)
    outgoing = jnp.einsum("rs,rd->sd", place, moe_in, preferred_element_type=jnp.float32).astype(
        jnp.bfloat16
    )
    expert_gu = gate_up[0]
    expert_down = down[0]
    packed = outgoing.reshape(experts, slots_each, width)
    block = lax.all_to_all(packed, ("seq", "tp"), split_axis=0, concat_axis=0, tiled=True)
    result = expert_ffn(block.reshape(-1, width), expert_gu, expert_down)
    processed = result.reshape(block.shape)
    returned = lax.all_to_all(processed, ("seq", "tp"), split_axis=0, concat_axis=0, tiled=True)
    returned = returned.reshape(experts * slots_each, width).astype(jnp.float32)
    experts_out = jnp.dot(weighted, returned, precision=lax.Precision.HIGHEST).astype(jnp.bfloat16)
    return (attended, experts_out)


def solution(mesh):
    placed = (
        P(("seq", "tp"), None),
        P(),
        P(),
        P("seq", "tp", None),
        P("seq", "tp", None),
        P("seq", "tp", None),
        P("tp", None),
        P(("seq", "tp"), None, None),
        P(("seq", "tp"), None, None),
        P(("seq", "tp"), None),
        P(("seq", "tp"), None),
    )
    return jax.shard_map(
        on_device,
        mesh=mesh,
        in_specs=placed,
        out_specs=(P(("seq", "tp"), None), P(("seq", "tp"), None)),
        check_vma=False,
    )
```

profile of v0, /device:TPU:1, one launch (start us, length us, event | category | flops | bytes accessed | tf_op | source)
XLA Modules:
  0.0 379.8 jit_solution(984537508272684308)
XLA Ops:
  11.6 25.6 %all_gather.13 = bf16[2880,1,128]{2,1,0:T(2,128)(2,1)} all-gather(bf16[180,1,128]{2,1,0:T(2,128)(2,1)S(1)} %copy.33), channel_id=1, replica_groups=mesh['seq'=16,'tp'=8] {'seq'}, dimensions={0}, use_global_device_ids=true | all-gather | bytes 783360 | tf_op jit(solution)/shard_map/all_gather | solution.py:78
  40.6 2.7 fusion.5
  46.3 3.4 collective-permute-start
  51.4 51.3 %all-gather.6.cloned.1.call-done = bf16[2880,1,512]{2,1,0:T(2,128)(2,1)} async-done(((bf16[180,1,512]{2,1,0:T(2,128)(2,1)}), bf16[2880,1,512]{2,1,0:T(2,128)(2,1)}) %all-gather.6.cloned.1.call-update) | async-done | bytes 2949136 | tf_op jit(solution)/shard_map/all_gather | solution.py:77
  102.8 13.5 %copy.47 = bf16[2880,1,512]{0,2,1:T(8,128)(2,1)} copy(bf16[2880,1,512]{2,1,0:T(2,128)(2,1)} %all-gather.6.cloned.1.call-done) | data formatting | bytes 5898240 | tf_op jit(solution)/shard_map/td,dhe->the/dot_general | solution.py:81
  116.2 3.8 fusion.22
  120.2 2.7 fusion.2
  123.1 2.8 fusion.27
  125.8 26.1 %all-gather.8.cloned.1.call-done = bf16[512,1,2880]{2,0,1:T(8,128)(2,1)} async-done(((bf16[32,1,2880]{2,0,1:T(8,128)(2,1)}), bf16[512,1,2880]{2,0,1:T(8,128)(2,1)}) %all-gather.8.cloned.1.call-update) | async-done | bytes 2949136 | tf_op jit(solution)/shard_map/all_gather | solution.py:79
  151.9 5.3 %convolution_convert_fusion.1 = bf16[512,2880]{1,0:T(8,128)(2,1)} fusion(bf16[512,512]{0,1:T(8,128)(2,1)S(1)} %bitcast.77, bf16[512,1,2880]{2,0,1:T(8,128)(2,1)} %all-gather.8.cloned.1.call-done), kind=kOutput, calls=%fused_computation.16 | convolution fusion | flops 1511424000 | bytes 6422528 | tf_op jit(solution)/shard_map/tjg,gjd->td/dot_general | solution.py:100
  158.3 8.4 %eq.43 = f32[256,128,4]{2,1,0:T(8,128)} broadcast(f32[256,128]{1,0:T(8,128)S(1)} %fusion.46), dimensions={0,1} | broadcast | bytes 655360 | tf_op jit(solution)/shard_map/eq | solution.py:114
  166.8 15.1 %eq.44 = f32[64,4,512]{2,1,0:T(4,128)S(1)} reshape(f32[256,128,4]{2,1,0:T(8,128)} %eq.43) | data formatting | bytes 1048576 | tf_op jit(solution)/shard_map/eq | solution.py:114
  182.0 8.4 %mul.208 = f32[256,128,4]{2,1,0:T(8,128)} broadcast(f32[256,128]{1,0:T(8,128)S(1)} %fusion.48), dimensions={0,1} | broadcast | bytes 655360 | tf_op jit(solution)/shard_map/mul | solution.py:114
  190.4 15.4 %mul.209 = f32[64,4,512]{2,1,0:T(4,128)S(1)} reshape(f32[256,128,4]{2,1,0:T(8,128)} %mul.208) | data formatting | bytes 1048576 | tf_op jit(solution)/shard_map/mul | solution.py:114
  206.7 16.6 %all-reduce.2.cloned.1.call-done = bf16[512,2880]{1,0:T(8,128)(2,1)} async-done(((bf16[512,2880]{1,0:T(8,128)(2,1)}), bf16[512,2880]{1,0:T(8,128)(2,1)}) %all-reduce.2.cloned.1.call-update) | async-done | bytes 2949136 | tf_op jit(solution)/shard_map/psum | solution.py:101
  225.6 3.0 copy.40
  228.7 4.7 %reshape.418 = bf16[128,4,2880]{2,1,0:T(4,128)(2,1)S(1)} reshape(bf16[512,2880]{1,0:T(8,128)(2,1)} %copy.40) | data formatting | bytes 5898240 | tf_op jit(solution)/shard_map/reshape | solution.py:123
  233.3 50.1 %all_to_all.10 = bf16[128,4,2880]{2,1,0:T(4,128)(2,1)} all-to-all(bf16[128,4,2880]{2,1,0:T(4,128)(2,1)S(1)} %reshape.418), channel_id=1, replica_groups=mesh['seq'=16,'tp'=8] {'seq','tp'}, dimensions={0} | all-to-all | bytes 5898240 | tf_op jit(solution)/shard_map/all_to_all | solution.py:124
  283.4 4.4 %reshape.419 = bf16[512,2880]{1,0:T(8,128)(2,1)S(1)} reshape(bf16[128,4,2880]{2,1,0:T(4,128)(2,1)} %all_to_all.10) | data formatting | bytes 5898240 | tf_op jit(solution)/shard_map/reshape | solution.py:125
  287.8 15.3 %fusion = f32[512,2880]{0,1:T(8,128)} fusion(bf16[512,2880]{1,0:T(8,128)(2,1)S(1)} %reshape.419, bf16[1,2880,2880]{2,1,0:T(8,128)(2,1)} %param.18), kind=kOutput, calls=%fused_computation | convolution fusion | flops 8493465600 | bytes 25436160 | tf_op jit(solution)/shard_map/dot_general | solution.py:51
  303.0 11.8 %fusion.10 = bf16[512,2880]{0,1:T(8,128)(2,1)} fusion(bf16[1,1440,2880]{2,1,0:T(8,128)(2,1)} %param.19, f32[512,2880]{0,1:T(8,128)} %fusion), kind=kOutput, calls=%fused_computation.14 | convolution fusion | flops 4254105600 | bytes 17141760 | tf_op jit(solution)/shard_map/dot_general | solution.py:55
  314.8 3.3 copy.41
  320.5 45.9 %all_to_all.11 = bf16[128,4,2880]{2,1,0:T(4,128)(2,1)} all-to-all(bf16[128,4,2880]{2,1,0:T(4,128)(2,1)} %reshape.420), channel_id=1, replica_groups=mesh['seq'=16,'tp'=8] {'seq','tp'}, dimensions={0} | all-to-all | bytes 5898240 | tf_op jit(solution)/shard_map/all_to_all | solution.py:127
  366.4 4.4 %reshape.421 = bf16[512,2880]{1,0:T(8,128)(2,1)S(1)} reshape(bf16[128,4,2880]{2,1,0:T(4,128)(2,1)} %all_to_all.11) | data formatting | bytes 5898240 | tf_op jit(solution)/shard_map/reshape | solution.py:128
  (66 shorter events, 21.9 us)
Async XLA Ops:
  7.2 33.4 %all-gather.4.cloned.1.call-start = ((), (), s32[]{:S(2)}) async-start(), calls=%async_computation.2 | async-start | bytes 3391488 | tf_op jit(solution)/shard_map/all_gather | solution.py:73
  7.9 94.9 %all-gather.6.cloned.1.call-start = ((), (), s32[]{:S(2)}) async-start(), calls=%async_computation.3 | async-start | bytes 6266880 | tf_op jit(solution)/shard_map/all_gather | solution.py:77
  9.9 33.4 %copy-start.10 = (f32[2880]{0:T(1024)S(1)}, f32[2880]{0:T(1024)}, u32[]{:S(2)}) copy-start(f32[2880]{0:T(1024)} %param.12) | copy-start | bytes 34564
  9.9 142.0 %all-gather.8.cloned.1.call-start = ((), (), s32[]{:S(2)}) async-start(), calls=%async_computation.4 | async-start | bytes 3203072 | tf_op jit(solution)/shard_map/all_gather | solution.py:79
  10.7 212.7 %all-reduce.2.cloned.1.call-start = ((), (), s32[]{:S(2)}) async-start(), calls=%async_computation.5 | async-start | bytes 6029312 | tf_op jit(solution)/shard_map/psum | solution.py:101
  40.6 2.8 copy-start
  43.3 2.6 copy-start.8
  43.3 6.3 %copy-start.11 = (f32[1,8]{1,0:T(1,128)S(1)}, f32[1,8]{1,0:T(1,128)}, u32[]{:S(2)}) copy-start(f32[1,8]{1,0:T(1,128)} %param.17) | copy-start | bytes 100
  46.3 4.5 %collective-permute-start = (bf16[128,1,128]{0,2,1:T(8,128)(2,1)S(1)}, bf16[128,1,128]{0,2,1:T(8,128)(2,1)S(1)}, u32[]{:S(2)}, u32[]{:S(2)}) collective-permute-start(bf16[128,1,128]{0,2,1:T(8,128)(2,1)S(1)} %fusion.65), channel_id=1, source_target_pairs={{0,8},{8,16},{16,24},{24,32},{32,40},{40,48},{48,56},{56,64},{64,7... | collective-permute-start | bytes 98312 | tf_op jit(solution)/shard_map/ppermute | solution.py:15
  116.2 4.0 %copy-start.4 = (bf16[128,1,64]{0,2,1:T(8,128)(2,1)S(1)}, bf16[128,1,64]{0,2,1:T(8,128)(2,1)}, u32[]{:S(2)}) copy-start(bf16[128,1,64]{0,2,1:T(8,128)(2,1)} %get-tuple-element.11) | copy-start | bytes 49156
  120.2 2.8 copy-start.9
  120.2 2.8 copy-start.3
  157.2 0.7 copy-start.6
  190.4 15.5 %copy-start.7 = (f32[64,4]{0,1:T(4,128)S(1)}, f32[64,4]{0,1:T(4,128)}, u32[]{:S(2)}) copy-start(f32[64,4]{0,1:T(4,128)} %param.21) | copy-start | bytes 3076
  190.4 32.9 %copy-start.1 = (bf16[64,2880]{1,0:T(8,128)(2,1)S(1)}, bf16[64,2880]{1,0:T(8,128)(2,1)}, u32[]{:S(2)}) copy-start(bf16[64,2880]{1,0:T(8,128)(2,1)} %param.11) | copy-start | bytes 1105924
  190.4 34.2 %copy-start.5 = (f32[2880]{0:T(1024)S(1)}, f32[2880]{0:T(1024)}, u32[]{:S(2)}) copy-start(f32[2880]{0:T(1024)} %param.13) | copy-start | bytes 34564
  224.6 4.1 %copy-start.2 = (bf16[64,2880]{1,0:T(8,128)(2,1)}, bf16[64,2880]{1,0:T(8,128)(2,1)S(1)}, u32[]{:S(2)}) copy-start(bf16[64,2880]{1,0:T(8,128)(2,1)S(1)} %get-tuple-element.5) | copy-start | bytes 1105924
Sparse Core Ops, SparseCore 0:
  9.7 30.8 all-gather.3
  43.3 59.3 all-gather.5
  104.9 46.9 all-gather.7
  157.3 65.9 all-reduce.1
where the time goes:
time: 381 us; the launch traced here: 380 us
  blocking collectives  122 us (32%)
  waiting for transfers between devices  97.9 us (26%)
  local copies, waits for them, and re-layouts  88.7 us (23%)
  matrix products  47.9 us (13%)
  between operations  14.1 us (4%)
  other arithmetic  6.01 us (2%)
    all_gather x1, waiting for transfers between devices, on_device(): lax.all_gather(q_weight, 'seq', axis=0, tiled=True)  51.3 us
    all_to_all x1, blocking collectives, on_device(): lax.all_to_all(packed, ('seq', 'tp'), split_axis=0, concat_axis=0, tiled=...  50.1 us
    all_to_all x1, blocking collectives, on_device(): lax.all_to_all(processed, ('seq', 'tp'), split_axis=0, concat_axis=0, til...  45.9 us
    all_gather x1, waiting for transfers between devices, on_device(): lax.all_gather(o_weight, 'seq', axis=0, tiled=True)  26.1 us
    all_gather x1, blocking collectives, on_device(): lax.all_gather(kv_weight, 'seq', axis=0, tiled=True)  25.6 us
    mul x2, local copies, waits for them, and re-layouts, on_device(): onehot[:, :, None]  23.8 us
    eq x4, local copies, waits for them, and re-layouts, on_device(): before[:, :, None] == ranks[None, None, :]  23.7 us
    psum x1, waiting for transfers between devices, on_device(): lax.psum(partial_value.astype(jnp.bfloat16), 'tp').astype(jnp.float32)  16.6 us
  transfers between devices with their start and end apart: 5, of which 4 were waited for; matrix products, arithmetic and copies ran while one was open for 22% of the time, Pallas kernels for 0%

commit v1 on v0

v1 whole, which is shorter than its diff:
```python
import functools

import jax
import jax.numpy as jnp
from jax import lax
from jax.experimental import pallas as pl
from jax.experimental.pallas import tpu as pltpu
from jax.sharding import Mesh
from jax.sharding import PartitionSpec as P

WINDOW = 128
ROPE_BASE = 150000.0
BF = jnp.bfloat16
F32 = jnp.float32
LOG2E = 1.4426950408889634
OFFSETS = (0, -1, 1, 2)
VMEM = pl.BlockSpec(memory_space=pltpu.VMEM)
SMEM = pl.BlockSpec(memory_space=pltpu.SMEM)
ANY = pl.BlockSpec(memory_space=pl.ANY)


def shifted(block, axis, distance):
    return lax.ppermute(block, axis, [(i, (i + distance) % 4) for i in range(4)])


def swapped(block):
    return lax.ppermute(block, "c", [(0, 1), (1, 0)])


def near(block, axis):
    return shifted(block, axis, 1), shifted(block, axis, -1)


def far(pair, axis, half):
    return shifted(pair[0][:half], axis, 1), shifted(pair[1][half:], axis, -1)


def rms_norm(values, gain):
    wide = values.astype(F32)
    scale = lax.rsqrt(jnp.mean(wide * wide, axis=-1, keepdims=True) + 1e-05)
    return (wide * scale * gain).astype(BF)


def params(limit):
    return pltpu.CompilerParams(vmem_limit_bytes=limit << 20)


def cost(flops, moved):
    return pl.CostEstimate(flops=flops, bytes_accessed=moved, transcendentals=0)


def shard_of(at_ref, first, second, first_is_x):
    dx, dz = (first, second) if first_is_x else (second, first)
    x = lax.rem(at_ref[0] + (OFFSETS[dx] + 4), 4)
    z = lax.rem(at_ref[1] + (OFFSETS[dz] + 4), 4)
    return x * 4 + z


def parts_of(refs):
    own, fore, back, far_a, far_b = refs
    for first in range(4):
        yield first, 0, own, first
        yield first, 1, fore, first
        yield first, 2, back, first
        yield first, 3, (far_a if first < 2 else far_b), first % 2


def rotated(values, cos, sin):
    lanes = values.shape[1]
    lane = lax.broadcasted_iota(jnp.int32, values.shape, 1)
    low = lax.rem(lane, 64) < 32
    other = jnp.where(low, pltpu.roll(values, lanes - 32, 1), pltpu.roll(values, 32, 1))
    return values * cos + other * sin


def row_starts(at_ref):
    for core in range(2):
        for offset in OFFSETS:
            y = lax.rem(at_ref[2] + (offset + 4), 4)
            c = at_ref[3] if core == 0 else 1 - at_ref[3]
            yield pl.multiple_of((y * 2 + c) * 64, 64)


def in_order(at_ref, ref):
    return jnp.concatenate([ref[pl.ds(start, 64), :] for start in row_starts(at_ref)], 0)


def fetched(pairs, sems):
    copies = [pltpu.make_async_copy(a, b, sems.at[i]) for i, (a, b) in enumerate(pairs)]
    for copy in copies:
        copy.start()
    for copy in copies:
        copy.wait()


def token_pairs(xo_ref, xs_ref, x_ref):
    for core, ref in enumerate((xo_ref, xs_ref)):
        for i in range(4):
            start = core * 256 + i * 64
            yield ref.at[i], x_ref.at[start : start + 64]


def weight_pairs(at_ref, refs, first_is_x, columns, w_ref):
    for first, second, ref, index in parts_of(refs):
        shard = shard_of(at_ref, first, second, first_is_x)
        yield ref.at[index, :, columns], w_ref.at[shard]


def projected(x_ref, w_ref):
    rows = x_ref.shape[1] // 16
    total = jnp.zeros((x_ref.shape[0], w_ref.shape[2]), F32)
    for s in range(16):
        x = x_ref[:, s * rows : (s + 1) * rows]
        total += jnp.dot(x, w_ref[s, :rows], preferred_element_type=F32)
    return total


def kv_kernel(at_ref, cos_ref, sin_ref, xo_ref, xs_ref, *refs):
    b_refs, (out_ref, x_ref, w_ref, sems) = refs[:5], refs[5:]
    pairs = list(token_pairs(xo_ref, xs_ref, x_ref))
    pairs += list(weight_pairs(at_ref, b_refs, False, slice(256, 384), w_ref))
    fetched(pairs, sems)
    total = projected(x_ref, w_ref)
    lane = lax.broadcasted_iota(jnp.int32, total.shape, 1)
    turned = rotated(total, in_order(at_ref, cos_ref), in_order(at_ref, sin_ref))
    result = jnp.where(lane < 64, turned, total).astype(BF)
    for i, start in enumerate(row_starts(at_ref)):
        out_ref[pl.ds(start, 64), :] = result[i * 64 : i * 64 + 64]


def q_kernel(at_ref, cos_ref, sin_ref, xo_ref, xs_ref, *refs):
    a_refs, b_refs, (out_ref, x_ref, wa_ref, wb_ref, sems) = refs[:5], refs[5:10], refs[10:]
    pairs = list(token_pairs(xo_ref, xs_ref, x_ref))
    pairs += list(weight_pairs(at_ref, a_refs, True, slice(0, 256), wa_ref))
    pairs += list(weight_pairs(at_ref, b_refs, False, slice(0, 256), wb_ref))
    fetched(pairs, sems)
    cos = jnp.concatenate([in_order(at_ref, cos_ref)] * 2, axis=1)
    sin = jnp.concatenate([in_order(at_ref, sin_ref)] * 2, axis=1)
    for half, w_ref in enumerate((wa_ref, wb_ref)):
        result = rotated(projected(x_ref, w_ref), cos, sin).astype(BF)
        for i, start in enumerate(row_starts(at_ref)):
            out_ref[pl.ds(start, 64), half * 256 : half * 256 + 256] = result[i * 64 : i * 64 + 64]


def attention_kernel(at_ref, q_ref, kv_ref, before_ref, sinks_ref, out_ref, all_ref):
    span = q_ref.shape[0]
    all_ref[:WINDOW] = before_ref[...]
    all_ref[WINDOW:] = kv_ref[...]
    shape = (4 * WINDOW, 2 * WINDOW)
    row = lax.rem(lax.broadcasted_iota(jnp.int32, shape, 0), WINDOW)
    column = lax.broadcasted_iota(jnp.int32, shape, 1)
    inside = (column > row) & (column <= row + WINDOW)
    is_first = (at_ref[0] == 0) & (at_ref[1] == 0)
    pair = lax.broadcasted_iota(jnp.int32, (4 * WINDOW, 1), 0) // WINDOW
    sink = []
    for odd in range(2):
        level = jnp.zeros((4 * WINDOW, 1), F32)
        for p in range(4):
            level = jnp.where(pair == p, sinks_ref[0, 2 * p + odd], level)
        sink.append(jnp.exp2(level * LOG2E - 20.0))
    for i in range(span // WINDOW):
        both = all_ref[i * WINDOW : (i + 2) * WINDOW]
        zero = jnp.zeros((2 * WINDOW, 64), BF)
        key, value = both[:, :64], both[:, 64:]
        keys = jnp.concatenate(
            [jnp.concatenate([key, zero], 1), jnp.concatenate([zero, key], 1)], 0
        )
        values = jnp.concatenate(
            [jnp.concatenate([value, zero], 1), jnp.concatenate([zero, value], 1)], 0
        )
        query = jnp.concatenate(
            [q_ref[i * WINDOW : (i + 1) * WINDOW, p * 128 : (p + 1) * 128] for p in range(4)], 0
        )
        scores = lax.dot_general(
            query, keys, (((1,), (1,)), ((), ())), preferred_element_type=F32
        )
        allowed = inside
        if i == 0:
            allowed = inside & ((column >= WINDOW) | jnp.logical_not(is_first))
        probs = []
        for odd in range(2):
            part = scores[:, odd * 256 : odd * 256 + 256]
            expo = jnp.where(allowed, jnp.exp2(part * (0.125 * LOG2E) - 20.0), 0.0)
            denom = jnp.sum(expo, axis=1, keepdims=True) + sink[odd]
            probs.append((expo * (1.0 / denom)).astype(BF))
        out = jnp.dot(jnp.concatenate(probs, 1), values, preferred_element_type=F32).astype(BF)
        for p in range(4):
            out_ref[i * WINDOW : (i + 1) * WINDOW, p * 128 : (p + 1) * 128] = out[
                p * WINDOW : (p + 1) * WINDOW
            ]


def head_rows(at_ref, heads_ref, is_other):
    c = 1 - at_ref[3] if is_other else at_ref[3]
    rows = []
    for step in range(4):
        start = (lax.rem(at_ref[2] + step, 4) * 2 + c) * 64
        rows.append(heads_ref[pl.ds(pl.multiple_of(start, 64), 64), :])
    return jnp.concatenate(rows, 0)


def other_kernel(at_ref, heads_ref, w_ref, out_ref):
    rows = head_rows(at_ref, heads_ref, True)
    total = jnp.dot(rows, w_ref[...], preferred_element_type=F32).astype(BF)
    for i in range(4):
        out_ref[i] = total[i * 64 : i * 64 + 64]


def own_kernel(at_ref, heads_ref, w_ref, got_ref, up_ref, down_ref, one_ref, three_ref, zero_ref):
    rows = head_rows(at_ref, heads_ref, False)
    total = jnp.dot(rows, w_ref[...], preferred_element_type=F32)
    block = lambda i: total[i * 64 : i * 64 + 64] + got_ref[i].astype(F32)
    far_block = block(2).astype(BF)
    up_ref[...] = far_block[:32]
    down_ref[...] = far_block[32:]
    one_ref[...] = block(1)
    three_ref[...] = block(3)
    zero_ref[...] = block(0)


def dispatch_kernel(place_ref, own_ref, other_ref, out_ref):
    rows = jnp.concatenate([own_ref[...], other_ref[...]], 0)
    out_ref[...] = jnp.dot(place_ref[...], rows, preferred_element_type=F32).astype(BF)


def combine_kernel(weights_ref, rows_ref, own_ref, other_ref):
    both = jnp.dot(weights_ref[...], rows_ref[...], preferred_element_type=F32)
    total = both[:128] + both[128:]
    own_ref[...] = total[:64]
    other_ref[...] = total[64:]


TILE = 512


def activate(both_ref, act_ref, first, last, width):
    for start in range(0, both_ref.shape[0], 64):
        rows = slice(start, start + 64)
        gate = both_ref[rows, first:last]
        upper = both_ref[rows, width + first : width + last]
        act_ref[rows, first:last] = ((upper + 1.0) * gate * jax.nn.sigmoid(1.702 * gate)).astype(BF)


def expert_kernel(steps, width, rows_ref, gu_ref, down_ref, out_ref, both_ref, act_ref):
    step = pl.program_id(0)
    ready = {}
    for first in range(0, width, TILE):
        last = min(first + TILE, width)
        ready.setdefault((width + last - 1) // TILE + 1, []).append((first, last))

    for i in range(steps):

        @pl.when(step == i)
        def _():
            both_ref[:, i * TILE : (i + 1) * TILE] = jnp.dot(
                rows_ref[...], gu_ref[0], preferred_element_type=F32
            )
            for first, last in ready.get(i, ()):
                activate(both_ref, act_ref, first, last, width)

    @pl.when(step == steps)
    def _():
        for first, last in ready.get(steps, ()):
            activate(both_ref, act_ref, first, last, width)

    @pl.when(step >= steps)
    def _():
        out_ref[...] = jnp.dot(act_ref[...], down_ref[0], preferred_element_type=F32).astype(BF)


def expert_ffn(rows, gate_up, down):
    count, model = rows.shape
    width = down.shape[1]
    steps = pl.cdiv(2 * width, TILE)
    return pl.pallas_call(
        functools.partial(expert_kernel, steps, width),
        grid=(steps + pl.cdiv(model, TILE),),
        out_shape=jax.ShapeDtypeStruct((count, model), BF),
        in_specs=[
            pl.BlockSpec((count, model), lambda i: (0, 0)),
            pl.BlockSpec((1, model, TILE), lambda i: (0, 0, jnp.minimum(i, steps - 1))),
            pl.BlockSpec((1, width, TILE), lambda i: (0, 0, jnp.maximum(i - steps, 0))),
        ],
        out_specs=pl.BlockSpec((count, TILE), lambda i: (0, jnp.maximum(i - steps, 0))),
        scratch_shapes=[
            pltpu.VMEM((count, steps * TILE), F32),
            pltpu.VMEM((count, width), BF),
        ],
        compiler_params=params(56),
        cost_estimate=cost(2 * count * model * 3 * width, 31_000_000),
        name="experts",
    )(rows, gate_up, down)


def routing(ids, weights, core, slots, experts):
    count = ids.shape[1]
    total = experts // 2 * 2 * slots
    slot = jnp.arange(total, dtype=jnp.int32)[:, None]
    expert = slot // (2 * slots) * 2 + core
    token = jnp.arange(count, dtype=jnp.int32)
    named = jnp.zeros((total, count), F32)
    weight = jnp.zeros((total, count), F32)
    for j in range(ids.shape[0]):
        same = ids[j][None, :] == expert
        named = named + same.astype(F32)
        weight = weight + jnp.where(same, weights[j][None, :], 0.0)
    half = count // 2
    earlier = (token[:, None] < token[None, :]) & (token[:, None] // half == token[None, :] // half)
    rank = jnp.dot(named.astype(BF), earlier.astype(BF), preferred_element_type=F32)
    here = (rank == (slot % slots).astype(F32)) & (slot // slots % 2 == token[None, :] // half)
    place = jnp.where(here, named, 0.0).astype(BF)
    weighted = jnp.where(here, weight, 0.0).T
    high = lax.reduce_precision(weighted, 8, 7)
    return place, jnp.concatenate([high, weighted - high], 0).astype(BF)


def on_device(
    tokens, attn_gain, moe_gain, q_weight, kv_weight, o_weight, sinks, gate_up, down, expert_ids, route_weights
):
    rows, width = tokens.shape
    barrier = lax.optimization_barrier
    at = jnp.stack([lax.axis_index(a) for a in ("x", "z", "y", "c")]).astype(jnp.int32)

    normed = rms_norm(tokens, attn_gain)
    o_all = lax.all_gather(o_weight[:, 0, :], ("x", "z"), axis=0, tiled=True)
    span = 8 * rows

    q2, kv2 = q_weight[:, 0, :], kv_weight[:, 0, :]
    padded = lambda array: jnp.pad(array, ((0, 4), (0, 0)))
    qa, qb = padded(q2[:, :256]), padded(jnp.concatenate([q2[:, 256:], kv2], axis=1))
    stack = lambda own, pair, rest: jnp.stack([own, *pair, jnp.concatenate(rest)])
    na, nb = near(qa, "x"), near(qb, "z")
    fa, fb = far(na, "x", 96), far(nb, "z", 96)
    sa, sb = stack(qa, na, fa), stack(qb, nb, fb)
    na, nb = near(sa, "z"), near(sb, "x")
    x_parts = (normed, *near(normed, "y"), shifted(normed, "y", 2))
    x_parts = barrier((*x_parts, *na, *nb))[:4]
    x_own = jnp.stack(x_parts)
    x_other = swapped(x_own)
    fa, fb = far(na, "z", 2), far(nb, "x", 2)
    a_parts, b_parts = (sa, *na, *fa), (sb, *nb, *fb)

    half = 32
    freq = ROPE_BASE ** (-(jnp.arange(half, dtype=F32) * 2.0) / (2.0 * half))
    first = (at[0] * 4 + at[1]) * span
    angle = (first + jnp.arange(span, dtype=jnp.int32)).astype(F32)[:, None] * freq
    cos, sin = jnp.cos(angle), jnp.sin(angle)
    cos = jnp.concatenate([cos] * 4, axis=1)
    sin = jnp.concatenate([-sin, sin, -sin, sin], axis=1)

    mine = jnp.concatenate([expert_ids.astype(F32), route_weights], axis=1)
    theirs = swapped(mine)
    table = jnp.concatenate([mine, theirs], axis=0).T
    topk = expert_ids.shape[1]
    place, weighted = routing(table[:topk].astype(jnp.int32), table[topk:], at[3], 4, 128)
    at, place, weighted = barrier((at, place, weighted))

    shard = qa.shape[0]
    x_scratch = pltpu.VMEM((span, width), BF)
    kv = pl.pallas_call(
        kv_kernel,
        out_shape=jax.ShapeDtypeStruct((span, 128), BF),
        in_specs=[SMEM] + [VMEM] * 2 + [ANY] * 7,
        out_specs=VMEM,
        scratch_shapes=[x_scratch, pltpu.VMEM((16, shard, 128), BF), pltpu.SemaphoreType.DMA((24,))],
        compiler_params=params(16),
        cost_estimate=cost(2 * span * width * 128, 8_000_000),
        name="keyval",
    )(at, cos, sin, x_own, x_other, *b_parts)
    before = lax.ppermute(kv[span - WINDOW :], ("x", "z"), [(i, i + 1) for i in range(15)])
    query = pl.pallas_call(
        q_kernel,
        out_shape=jax.ShapeDtypeStruct((span, 512), BF),
        in_specs=[SMEM] + [VMEM] * 2 + [ANY] * 12,
        out_specs=VMEM,
        scratch_shapes=[x_scratch]
        + [pltpu.VMEM((16, shard, 256), BF)] * 2
        + [pltpu.SemaphoreType.DMA((40,))],
        compiler_params=params(20),
        cost_estimate=cost(2 * span * width * 512, 8_000_000),
        name="query",
    )(at, cos, sin, x_own, x_other, *a_parts, *b_parts)
    heads = pl.pallas_call(
        attention_kernel,
        out_shape=jax.ShapeDtypeStruct((span, 512), BF),
        in_specs=[SMEM] + [VMEM] * 3 + [SMEM],
        out_specs=VMEM,
        scratch_shapes=[pltpu.VMEM((span + WINDOW, 128), BF)],
        compiler_params=params(12),
        cost_estimate=cost(4_000_000_000, 2_000_000),
        name="attention",
    )(at, query, kv, before, sinks)
    tile = 768
    steps = pl.cdiv(width, tile)
    columns = lambda count: pl.BlockSpec((count, tile), lambda i: (0, i))
    blocks = pl.BlockSpec((4, rows, tile), lambda i: (0, 0, i))
    common = [SMEM, pl.BlockSpec((span, 512), lambda i: (0, 0)), columns(512)]
    shape = lambda dtype, *dims: jax.ShapeDtypeStruct((*dims, width), dtype)
    other = pl.pallas_call(
        other_kernel,
        grid=(steps,),
        out_shape=shape(BF, 4, rows),
        in_specs=common,
        out_specs=blocks,
        compiler_params=params(16),
        cost_estimate=cost(span * width * 512, 5_000_000),
        name="other",
    )(at, heads, o_all)
    up, down_, one, three, zero = pl.pallas_call(
        own_kernel,
        grid=(steps,),
        out_shape=[shape(BF, 32)] * 2 + [shape(F32, rows)] * 3,
        in_specs=common + [blocks],
        out_specs=[columns(32)] * 2 + [columns(rows)] * 3,
        compiler_params=params(16),
        cost_estimate=cost(span * width * 512, 8_000_000),
        name="own",
    )(at, heads, o_all, swapped(other))
    wide = lambda array: array.astype(F32)
    up, down_ = shifted(up, "y", 1), shifted(down_, "y", -1)
    ahead = jnp.concatenate([one[:32] + wide(up), one[32:]]).astype(BF)
    behind = jnp.concatenate([three[:32], three[32:] + wide(down_)]).astype(BF)
    left, right = shifted(ahead, "y", 1), shifted(behind, "y", -1)
    attended = (wide(tokens) + (zero + wide(left) + wide(right))).astype(BF)
    moe_in = rms_norm(attended, moe_gain)

    slots = place.shape[0]
    outgoing = pl.pallas_call(
        dispatch_kernel,
        out_shape=jax.ShapeDtypeStruct((slots, width), BF),
        in_specs=[VMEM] * 3,
        out_specs=VMEM,
        compiler_params=params(12),
        name="dispatch",
    )(place, moe_in, swapped(moe_in))
    exchange = lambda array: lax.all_to_all(
        array.reshape(64, 8, width), ("x", "z", "y"), split_axis=0, concat_axis=0, tiled=True
    ).reshape(slots, width)
    result = expert_ffn(exchange(outgoing), gate_up, down)
    mine_out, their_out = pl.pallas_call(
        combine_kernel,
        out_shape=[jax.ShapeDtypeStruct((rows, width), F32)] * 2,
        in_specs=[VMEM] * 2,
        out_specs=[VMEM] * 2,
        compiler_params=params(12),
        name="combine",
    )(weighted, exchange(result))
    return attended, (mine_out + swapped(their_out)).astype(BF)


def solution(mesh):
    fine = Mesh(mesh.devices.reshape(4, 4, 4, 2), ("x", "z", "y", "c"))
    seq, tp, every = ("x", "z"), ("y", "c"), ("x", "z", "y", "c")
    placed = (
        P(every, None),
        P(),
        P(),
        P(seq, tp, None),
        P(seq, tp, None),
        P(seq, tp, None),
        P(tp, None),
        P(every, None, None),
        P(every, None, None),
        P(every, None),
        P(every, None),
    )
    return jax.shard_map(
        on_device,
        mesh=fine,
        in_specs=placed,
        out_specs=(P(every, None), P(every, None)),
        check_vma=False,
    )
```

time: 381 us -> 250 us (0.66)
  local copies, waits for them, and re-layouts: 88.7 us -> 3.14 us
  waiting for transfers between devices: 97.9 us -> 36.9 us
  matrix products: 47.9 us -> 1.05 us
  starting transfers between devices: 3.52 us -> 50.1 us
  Pallas kernels: 0 us -> 45.6 us
  blocking collectives: 122 us -> 90.9 us
    all_gather x3 -> x1, waiting for transfers between devices: 80 us -> 0.02 us  [on_device(): o_all = lax.all_gather(o_weight[:, 0, :], ('x', 'z'), axis=0, tiled=True)]
    dot_general x10 -> x1, matrix products: 47.9 us -> 1.05 us  [routing(): jnp.dot(named.astype(BF), earlier.astype(BF), preferred_element_type=F32)]
    ppermute x1 -> x29, starting transfers between devices: 3.36 us -> 50 us  [the longest x23 34.2 us: shifted(): lax.ppermute(block, axis, [(i, (i + distance) % 4) for i in range(4)])]
    pallas_call x0 -> x8, Pallas kernels: none -> 45.6 us  [the longest x1 23.6 us: expert_ffn(): pl.pallas_call(functools.partial(expert_kernel, steps, width), grid=(step...]
    ppermute x1 -> x29, waiting for transfers between devices: 0.01 us -> 36.2 us  [the longest x23 30.2 us: shifted(): lax.ppermute(block, axis, [(i, (i + distance) % 4) for i in range(4)])]
    all_gather x1 -> x0, blocking collectives: 25.6 us -> none  [on_device(): lax.all_gather(kv_weight, 'seq', axis=0, tiled=True)]
    mul x2 -> x0, local copies, waits for them, and re-layouts: 23.8 us -> none  [on_device(): onehot[:, :, None]]
    eq x5 -> x1, local copies, waits for them, and re-layouts: 23.8 us -> 0.01 us  [routing(): same = ids[j][None, :] == expert]
  transfers between devices with their start and end apart: 5 -> 30, of which waited for: 4 -> 11; matrix products, arithmetic and copies ran while one was open for 22% -> 3% of each run, Pallas kernels for 0% -> 6%
where the time goes in v1:
time: 250 us; the launch traced here: 249 us
  blocking collectives  90.9 us (36%)
  starting transfers between devices  50.1 us (20%)
  Pallas kernels  45.6 us (18%)
  waiting for transfers between devices  36.9 us (15%)
  between operations  14.5 us (6%)
  other arithmetic  6.93 us (3%)
  local copies, waits for them, and re-layouts  3.14 us (1%)
    all_to_all x2, blocking collectives, on_device(): lax.all_to_all(array.reshape(64, 8, width), ('x', 'z', 'y'), split_axis=0...  90.9 us
    ppermute x23, starting transfers between devices, shifted(): lax.ppermute(block, axis, [(i, (i + distance) % 4) for i in range(4)])  34.2 us
    ppermute x23, waiting for transfers between devices, shifted(): lax.ppermute(block, axis, [(i, (i + distance) % 4) for i in range(4)])  30.2 us
    pallas_call x1, Pallas kernels, expert_ffn(): pl.pallas_call(functools.partial(expert_kernel, steps, width), grid=(step...  23.6 us
    ppermute x5, starting transfers between devices, swapped(): return lax.ppermute(block, 'c', [(0, 1), (1, 0)])  14.5 us
    pallas_call x1, Pallas kernels, on_device(): pl.pallas_call(q_kernel, out_shape=jax.ShapeDtypeStruct((span, 512), BF),...  7.85 us
    ppermute x5, waiting for transfers between devices, swapped(): return lax.ppermute(block, 'c', [(0, 1), (1, 0)])  6.01 us
  transfers between devices with their start and end apart: 30, of which 11 were waited for; matrix products, arithmetic and copies ran while one was open for 3% of the time, Pallas kernels for 6%

profile of v1, /device:TPU:1, one launch (start us, length us, event | category | flops | bytes accessed | tf_op | source)
XLA Modules:
  0.0 249.1 jit_solution(12773860935651892182)
XLA Ops:
  8.9 3.4 %collective-permute-start.5 = (bf16[184,256]{1,0:T(8,128)(2,1)S(1)}, bf16[184,256]{1,0:T(8,128)(2,1)S(1)}, u32[]{:S(2)}, u32[]{:S(2)}) collective-permute-start(bf16[184,256]{1,0:T(8,128)(2,1)S(1)} %get-tuple-element.37), channel_id=1, source_target_pairs={{0,96},{32,0},{64,32},{96,64},{1,97},{33,1},{65,33},{97,65},{2,98}... | collective-permute-start | bytes 282632 | tf_op jit(solution)/shard_map/ppermute | solution.py:23
  13.1 3.8 %collective-permute-start.11 = (bf16[184,384]{1,0:T(8,128)(2,1)S(1)}, bf16[184,384]{1,0:T(8,128)(2,1)S(1)}, u32[]{:S(2)}, u32[]{:S(2)}) collective-permute-start(bf16[184,384]{1,0:T(8,128)(2,1)S(1)} %get-tuple-element.35), channel_id=1, source_target_pairs={{0,24},{8,0},{16,8},{24,16},{1,25},{9,1},{17,9},{25,17},{2,26},{10... | collective-permute-start | bytes 423944 | tf_op jit(solution)/shard_map/ppermute | solution.py:23
  19.4 2.7 %collective-permute-start.7 = (bf16[88,256]{1,0:T(8,128)(2,1)S(1)}, bf16[88,256]{1,0:T(8,128)(2,1)S(1)}, u32[]{:S(2)}, u32[]{:S(2)}) collective-permute-start(bf16[88,256]{1,0:T(8,128)(2,1)S(1)} %slice.105), channel_id=1, source_target_pairs={{0,96},{32,0},{64,32},{96,64},{1,97},{33,1},{65,33},{97,65},{2,98}... | collective-permute-start | bytes 135176 | tf_op jit(solution)/shard_map/ppermute | solution.py:23
  23.8 2.7 %collective-permute-start.13 = (bf16[88,384]{1,0:T(8,128)(2,1)S(1)}, bf16[88,384]{1,0:T(8,128)(2,1)S(1)}, u32[]{:S(2)}, u32[]{:S(2)}) collective-permute-start(bf16[88,384]{1,0:T(8,128)(2,1)S(1)} %slice.108), channel_id=1, source_target_pairs={{0,24},{8,0},{16,8},{24,16},{1,25},{9,1},{17,9},{25,17},{2,26},{10... | collective-permute-start | bytes 202760 | tf_op jit(solution)/shard_map/ppermute | solution.py:23
  28.4 2.7 %collective-permute-done.12 = bf16[96,384]{1,0:T(8,128)(2,1)S(1)} collective-permute-done((bf16[96,384]{1,0:T(8,128)(2,1)S(1)}, bf16[96,384]{1,0:T(8,128)(2,1)S(1)}, u32[]{:S(2)}, u32[]{:S(2)}) %collective-permute-start.12) | collective-permute-done | bytes 73760 | tf_op jit(solution)/shard_map/ppermute | solution.py:23
  31.3 3.7 %collective-permute-start.15 = (bf16[4,184,384]{2,1,0:T(8,128)(2,1)S(1)}, bf16[4,184,384]{2,1,0:T(8,128)(2,1)S(1)}, u32[]{:S(2)}, u32[]{:S(2)}) collective-permute-start(bf16[4,184,384]{2,1,0:T(8,128)(2,1)S(1)} %pad_maximum_fusion.1.refs_5_.refs_0_), channel_id=1, source_target_pairs={{0,96},{32,0},{64,32},{96,64},{1,97},{33,1},{65,33},{97,65},{2,98}... | collective-permute-start | bytes 1695752 | tf_op jit(solution)/shard_map/ppermute | solution.py:23
  35.1 2.7 %collective-permute-start.9 = (bf16[4,184,256]{2,1,0:T(8,128)(2,1)S(1)}, bf16[4,184,256]{2,1,0:T(8,128)(2,1)S(1)}, u32[]{:S(2)}, u32[]{:S(2)}) collective-permute-start(bf16[4,184,256]{2,1,0:T(8,128)(2,1)S(1)} %pad_maximum_fusion.2.refs_0_), channel_id=1, source_target_pairs={{0,24},{8,0},{16,8},{24,16},{1,25},{9,1},{17,9},{25,17},{2,26},{10... | collective-permute-start | bytes 1130504 | tf_op jit(solution)/shard_map/ppermute | solution.py:23
  40.6 5.4 %collective-permute-done.3 = bf16[64,2880]{1,0:T(8,128)(2,1)S(1)} collective-permute-done((bf16[64,2880]{1,0:T(8,128)(2,1)}, bf16[64,2880]{1,0:T(8,128)(2,1)S(1)}, u32[]{:S(2)}, u32[]{:S(2)}) %collective-permute-start.3) | collective-permute-done | bytes 368672 | tf_op jit(solution)/shard_map/ppermute | solution.py:23
  46.0 5.5 %collective-permute-start = (f32[64,8]{0,1:T(8,128)S(1)}, f32[64,8]{0,1:T(8,128)S(1)}, u32[]{:S(2)}, u32[]{:S(2)}) collective-permute-start(f32[64,8]{0,1:T(8,128)S(1)} %pad_maximum_fusion.8), channel_id=1, source_target_pairs={{0,1},{1,0},{2,3},{3,2},{4,5},{5,4},{6,7},{7,6},{8,9},{9,8},{10,11... | collective-permute-start | bytes 6152 | tf_op jit(solution)/shard_map/ppermute | solution.py:27
  56.4 2.7 %collective-permute-start.18 = (bf16[2,184,256]{2,1,0:T(8,128)(2,1)S(1)}, bf16[2,184,256]{2,1,0:T(8,128)(2,1)S(1)}, u32[]{:S(2)}, u32[]{:S(2)}) collective-permute-start(bf16[2,184,256]{2,1,0:T(8,128)(2,1)S(1)} %slice.110), channel_id=1, source_target_pairs={{0,24},{8,0},{16,8},{24,16},{1,25},{9,1},{17,9},{25,17},{2,26},{10... | collective-permute-start | bytes 565256 | tf_op jit(solution)/shard_map/ppermute | solution.py:23
  59.3 3.7 %collective-permute-start.20 = (bf16[2,184,384]{2,1,0:T(8,128)(2,1)S(1)}, bf16[2,184,384]{2,1,0:T(8,128)(2,1)S(1)}, u32[]{:S(2)}, u32[]{:S(2)}) collective-permute-start(bf16[2,184,384]{2,1,0:T(8,128)(2,1)S(1)} %slice.112), channel_id=1, source_target_pairs={{0,96},{32,0},{64,32},{96,64},{1,97},{33,1},{65,33},{97,65},{2,98}... | collective-permute-start | bytes 847880 | tf_op jit(solution)/shard_map/ppermute | solution.py:23
  63.2 6.0 %collective-permute-done.19.refs_8_.refs_3_ = bf16[2,184,384]{2,1,0:T(8,128)(2,1)S(1)} collective-permute-done((bf16[2,184,384]{2,1,0:T(8,128)(2,1)S(1)}, bf16[2,184,384]{2,1,0:T(8,128)(2,1)S(1)}, u32[]{:S(2)}, u32[]{:S(2)}) %collective-permute-start.19) | collective-permute-done | bytes 282656 | tf_op jit(solution)/shard_map/ppermute | solution.py:23
  69.2 3.8 %keyval.1.kv_ref = bf16[512,128]{1,0:T(8,128)(2,1)S(1)} custom-call(s32[4]{0:T(128)S(1)} %pad_add_fusion.at_ref, f32[512,128]{1,0:T(8,128)S(1)} %get-tuple-element.55.cos_ref, f32[512,128]{1,0:T(8,128)S(1)} %get-tuple-element.56.sin_ref, bf16[4,64,2880]{2,1,0:T(8,128)(2,1)S(1)} %pad_maximum_fusion.xo_ref, ...), custom_call_target="tpu_custom_call" | custom-call | flops 377487360 | bytes 8000000 | tf_op jit(solution)/shard_map/keyval/pallas_call | solution.py:360
  74.4 7.9 %query.1.q_ref = bf16[512,512]{1,0:T(8,128)(2,1)S(1)} custom-call(s32[4]{0:T(128)S(1)} %pad_add_fusion.at_ref, f32[512,128]{1,0:T(8,128)S(1)} %get-tuple-element.55.cos_ref, f32[512,128]{1,0:T(8,128)S(1)} %get-tuple-element.56.sin_ref, bf16[4,64,2880]{2,1,0:T(8,128)(2,1)S(1)} %pad_maximum_fusion.xo_ref, ...), custom_call_target="tpu_custom_call" | custom-call | flops 1509949440 | bytes 8000000 | tf_op jit(solution)/shard_map/query/pallas_call | solution.py:371
  90.2 2.9 %collective-permute-done.22.got_ref = bf16[4,64,2880]{2,1,0:T(8,128)(2,1)S(1)} collective-permute-done((bf16[4,64,2880]{2,1,0:T(8,128)(2,1)S(1)}, bf16[4,64,2880]{2,1,0:T(8,128)(2,1)S(1)}, u32[]{:S(2)}, u32[]{:S(2)}) %collective-permute-start.22) | collective-permute-done | bytes 1474592 | tf_op jit(solution)/shard_map/ppermute | solution.py:27
  93.2 3.5 %own.1 = (bf16[32,2880]{1,0:T(8,128)(2,1)S(1)}, bf16[32,2880]{1,0:T(8,128)(2,1)S(1)}, f32[64,2880]{1,0:T(8,128)S(1)}, f32[64,2880]{1,0:T(8,128)S(1)}, f32[64,2880]{1,0:T(8,128)S(1)}) custom-call(s32[4]{0:T(128)S(1)} %pad_add_fusion.at_ref, bf16[512,512]{1,0:T(8,128)(2,1)S(1)} %attention.1.heads_ref, bf16[512,2880]{1,0:T(8,128)(2,1)S(1)} %bitcast.56, ...), custom_call_target="tpu_custom_call" | custom-call | flops 754974720 | bytes 8000000 | tf_op jit(solution)/shard_map/own/pallas_call | solution.py:409
  98.3 4.3 %collective-permute-done.25 = bf16[32,2880]{1,0:T(8,128)(2,1)S(1)} collective-permute-done((bf16[32,2880]{1,0:T(8,128)(2,1)S(1)}, bf16[32,2880]{1,0:T(8,128)(2,1)S(1)}, u32[]{:S(2)}, u32[]{:S(2)}) %collective-permute-start.25) | collective-permute-done | bytes 184352 | tf_op jit(solution)/shard_map/ppermute | solution.py:23
  105.5 6.7 %collective-permute-done.26 = bf16[64,2880]{1,0:T(8,128)(2,1)S(1)} collective-permute-done((bf16[64,2880]{1,0:T(8,128)(2,1)S(1)}, bf16[64,2880]{1,0:T(8,128)(2,1)S(1)}, u32[]{:S(2)}, u32[]{:S(2)}) %collective-permute-start.26) | collective-permute-done | bytes 368672 | tf_op jit(solution)/shard_map/ppermute | solution.py:23
  112.2 3.3 %collective-permute-done.24 = bf16[64,2880]{1,0:T(8,128)(2,1)S(1)} collective-permute-done((bf16[64,2880]{1,0:T(8,128)(2,1)S(1)}, bf16[64,2880]{1,0:T(8,128)(2,1)S(1)}, u32[]{:S(2)}, u32[]{:S(2)}) %collective-permute-start.24) | collective-permute-done | bytes 368672 | tf_op jit(solution)/shard_map/ppermute | solution.py:23
  116.0 2.7 %collective-permute-start.27 = (bf16[64,2880]{1,0:T(8,128)(2,1)S(1)}, bf16[64,2880]{1,0:T(8,128)(2,1)S(1)}, u32[]{:S(2)}, u32[]{:S(2)}) collective-permute-start(bf16[64,2880]{1,0:T(8,128)(2,1)S(1)} %fusion.2.own_ref), channel_id=1, source_target_pairs={{0,1},{1,0},{2,3},{3,2},{4,5},{5,4},{6,7},{7,6},{8,9},{9,8},{10,11... | collective-permute-start | bytes 1105928 | tf_op jit(solution)/shard_map/ppermute | solution.py:27
  121.0 46.4 %all_to_all.10 = bf16[64,8,2880]{2,1,0:T(8,128)(2,1)} all-to-all(bf16[64,8,2880]{2,1,0:T(8,128)(2,1)S(1)} %bitcast.54), channel_id=1, replica_groups=mesh['x'=4,'z'=4,'y'=4,'c'=2] {'x','z','y'}, dimensions={0} | all-to-all | bytes 5898240 | tf_op jit(solution)/shard_map/all_to_all | solution.py:436
  167.3 23.6 %experts.1 = bf16[512,2880]{1,0:T(8,128)(2,1)} custom-call(bf16[512,2880]{1,0:T(8,128)(2,1)} %bitcast.57, bf16[1,2880,2880]{2,1,0:T(8,128)(2,1)} %gu_ref.1, bf16[1,1440,2880]{2,1,0:T(8,128)(2,1)} %down_ref.1), custom_call_target="tpu_custom_call" | custom-call | flops 12740198400 | bytes 31000000 | tf_op jit(solution)/shard_map/experts/pallas_call | solution.py:275
  191.0 44.5 %all_to_all.11 = bf16[64,8,2880]{2,1,0:T(8,128)(2,1)S(1)} all-to-all(bf16[64,8,2880]{2,1,0:T(8,128)(2,1)} %bitcast.58), channel_id=1, replica_groups=mesh['x'=4,'z'=4,'y'=4,'c'=2] {'x','z','y'}, dimensions={0} | all-to-all | bytes 5898240 | tf_op jit(solution)/shard_map/all_to_all | solution.py:436
  236.5 3.1 %collective-permute-start.28 = (f32[64,2880]{1,0:T(8,128)S(1)}, f32[64,2880]{1,0:T(8,128)S(1)}, u32[]{:S(2)}, u32[]{:S(2)}) collective-permute-start(f32[64,2880]{1,0:T(8,128)S(1)} %get-tuple-element.29), channel_id=1, source_target_pairs={{0,1},{1,0},{2,3},{3,2},{4,5},{5,4},{6,7},{7,6},{8,9},{9,8},{10,11... | collective-permute-start | bytes 2211848 | tf_op jit(solution)/shard_map/ppermute | solution.py:27
  (113 shorter events, 36.8 us)
Async XLA Ops:
  7.2 77.4 %all-gather.3.cloned.1.call-start = ((), (), s32[]{:S(2)}) async-start(), calls=%async_computation.2 | async-start | bytes 3203072 | tf_op jit(solution)/shard_map/all_gather | solution.py:325
  8.9 10.5 %collective-permute-start.5 = (bf16[184,256]{1,0:T(8,128)(2,1)S(1)}, bf16[184,256]{1,0:T(8,128)(2,1)S(1)}, u32[]{:S(2)}, u32[]{:S(2)}) collective-permute-start(bf16[184,256]{1,0:T(8,128)(2,1)S(1)} %get-tuple-element.37), channel_id=1, source_target_pairs={{0,96},{32,0},{64,32},{96,64},{1,97},{33,1},{65,33},{97,65},{2,98}... | collective-permute-start | bytes 282632 | tf_op jit(solution)/shard_map/ppermute | solution.py:23
  12.3 9.9 %collective-permute-start.4 = (bf16[184,256]{1,0:T(8,128)(2,1)S(1)}, bf16[184,256]{1,0:T(8,128)(2,1)S(1)}, u32[]{:S(2)}, u32[]{:S(2)}) collective-permute-start(bf16[184,256]{1,0:T(8,128)(2,1)S(1)} %get-tuple-element.37), channel_id=1, source_target_pairs={{0,32},{32,64},{64,96},{96,0},{1,33},{33,65},{65,97},{97,1},{2,34}... | collective-permute-start | bytes 282632 | tf_op jit(solution)/shard_map/ppermute | solution.py:23
  13.1 9.2 %collective-permute-start.11 = (bf16[184,384]{1,0:T(8,128)(2,1)S(1)}, bf16[184,384]{1,0:T(8,128)(2,1)S(1)}, u32[]{:S(2)}, u32[]{:S(2)}) collective-permute-start(bf16[184,384]{1,0:T(8,128)(2,1)S(1)} %get-tuple-element.35), channel_id=1, source_target_pairs={{0,24},{8,0},{16,8},{24,16},{1,25},{9,1},{17,9},{25,17},{2,26},{10... | collective-permute-start | bytes 423944 | tf_op jit(solution)/shard_map/ppermute | solution.py:23
  16.9 6.9 %collective-permute-start.10 = (bf16[184,384]{1,0:T(8,128)(2,1)S(1)}, bf16[184,384]{1,0:T(8,128)(2,1)S(1)}, u32[]{:S(2)}, u32[]{:S(2)}) collective-permute-start(bf16[184,384]{1,0:T(8,128)(2,1)S(1)} %get-tuple-element.35), channel_id=1, source_target_pairs={{0,8},{8,16},{16,24},{24,0},{1,9},{9,17},{17,25},{25,1},{2,10},{10... | collective-permute-start | bytes 423944 | tf_op jit(solution)/shard_map/ppermute | solution.py:23
  18.0 17.1 %collective-permute-start.1 = (bf16[64,2880]{1,0:T(8,128)(2,1)}, bf16[64,2880]{1,0:T(8,128)(2,1)}, u32[]{:S(2)}, u32[]{:S(2)}) collective-permute-start(bf16[64,2880]{1,0:T(8,128)(2,1)} %fusion.5), channel_id=1, source_target_pairs={{0,2},{2,4},{4,6},{6,0},{1,3},{3,5},{5,7},{7,1},{8,10},{10,12},{12... | collective-permute-start | bytes 1105928 | tf_op jit(solution)/shard_map/ppermute | solution.py:23
  19.4 7.2 %collective-permute-start.7 = (bf16[88,256]{1,0:T(8,128)(2,1)S(1)}, bf16[88,256]{1,0:T(8,128)(2,1)S(1)}, u32[]{:S(2)}, u32[]{:S(2)}) collective-permute-start(bf16[88,256]{1,0:T(8,128)(2,1)S(1)} %slice.105), channel_id=1, source_target_pairs={{0,96},{32,0},{64,32},{96,64},{1,97},{33,1},{65,33},{97,65},{2,98}... | collective-permute-start | bytes 135176 | tf_op jit(solution)/shard_map/ppermute | solution.py:23
  22.3 15.5 %collective-permute-start.2 = (bf16[64,2880]{1,0:T(8,128)(2,1)}, bf16[64,2880]{1,0:T(8,128)(2,1)}, u32[]{:S(2)}, u32[]{:S(2)}) collective-permute-start(bf16[64,2880]{1,0:T(8,128)(2,1)} %fusion.5), channel_id=1, source_target_pairs={{0,6},{2,0},{4,2},{6,4},{1,7},{3,1},{5,3},{7,5},{8,14},{10,8},{12,... | collective-permute-start | bytes 1105928 | tf_op jit(solution)/shard_map/ppermute | solution.py:23
  31.2 20.3 %collective-permute-start.14 = (bf16[4,184,384]{2,1,0:T(8,128)(2,1)S(1)}, bf16[4,184,384]{2,1,0:T(8,128)(2,1)S(1)}, u32[]{:S(2)}, u32[]{:S(2)}) collective-permute-start(bf16[4,184,384]{2,1,0:T(8,128)(2,1)S(1)} %pad_maximum_fusion.1.refs_5_.refs_0_), channel_id=1, source_target_pairs={{0,32},{32,64},{64,96},{96,0},{1,33},{33,65},{65,97},{97,1},{2,34}... | collective-permute-start | bytes 1695752 | tf_op jit(solution)/shard_map/ppermute | solution.py:23
  31.3 20.2 %collective-permute-start.15 = (bf16[4,184,384]{2,1,0:T(8,128)(2,1)S(1)}, bf16[4,184,384]{2,1,0:T(8,128)(2,1)S(1)}, u32[]{:S(2)}, u32[]{:S(2)}) collective-permute-start(bf16[4,184,384]{2,1,0:T(8,128)(2,1)S(1)} %pad_maximum_fusion.1.refs_5_.refs_0_), channel_id=1, source_target_pairs={{0,96},{32,0},{64,32},{96,64},{1,97},{33,1},{65,33},{97,65},{2,98}... | collective-permute-start | bytes 1695752 | tf_op jit(solution)/shard_map/ppermute | solution.py:23
  35.0 16.5 %collective-permute-start.8 = (bf16[4,184,256]{2,1,0:T(8,128)(2,1)S(1)}, bf16[4,184,256]{2,1,0:T(8,128)(2,1)S(1)}, u32[]{:S(2)}, u32[]{:S(2)}) collective-permute-start(bf16[4,184,256]{2,1,0:T(8,128)(2,1)S(1)} %pad_maximum_fusion.2.refs_0_), channel_id=1, source_target_pairs={{0,8},{8,16},{16,24},{24,0},{1,9},{9,17},{17,25},{25,1},{2,10},{10... | collective-permute-start | bytes 1130504 | tf_op jit(solution)/shard_map/ppermute | solution.py:23
  35.1 16.4 %collective-permute-start.9 = (bf16[4,184,256]{2,1,0:T(8,128)(2,1)S(1)}, bf16[4,184,256]{2,1,0:T(8,128)(2,1)S(1)}, u32[]{:S(2)}, u32[]{:S(2)}) collective-permute-start(bf16[4,184,256]{2,1,0:T(8,128)(2,1)S(1)} %pad_maximum_fusion.2.refs_0_), channel_id=1, source_target_pairs={{0,24},{8,0},{16,8},{24,16},{1,25},{9,1},{17,9},{25,17},{2,26},{10... | collective-permute-start | bytes 1130504 | tf_op jit(solution)/shard_map/ppermute | solution.py:23
  37.8 8.2 %collective-permute-start.3 = (bf16[64,2880]{1,0:T(8,128)(2,1)}, bf16[64,2880]{1,0:T(8,128)(2,1)S(1)}, u32[]{:S(2)}, u32[]{:S(2)}) collective-permute-start(bf16[64,2880]{1,0:T(8,128)(2,1)} %fusion.5), channel_id=1, source_target_pairs={{0,4},{2,6},{4,0},{6,2},{1,5},{3,7},{5,1},{7,3},{8,12},{10,14},{12... | collective-permute-start | bytes 1105928 | tf_op jit(solution)/shard_map/ppermute | solution.py:23
  46.0 9.1 %collective-permute-start = (f32[64,8]{0,1:T(8,128)S(1)}, f32[64,8]{0,1:T(8,128)S(1)}, u32[]{:S(2)}, u32[]{:S(2)}) collective-permute-start(f32[64,8]{0,1:T(8,128)S(1)} %pad_maximum_fusion.8), channel_id=1, source_target_pairs={{0,1},{1,0},{2,3},{3,2},{4,5},{5,4},{6,7},{7,6},{8,9},{9,8},{10,11... | collective-permute-start | bytes 6152 | tf_op jit(solution)/shard_map/ppermute | solution.py:27
  53.0 16.2 %collective-permute-start.16 = (bf16[4,64,2880]{2,1,0:T(8,128)(2,1)S(1)}, bf16[4,64,2880]{2,1,0:T(8,128)(2,1)S(1)}, u32[]{:S(2)}, u32[]{:S(2)}) collective-permute-start(bf16[4,64,2880]{2,1,0:T(8,128)(2,1)S(1)} %pad_maximum_fusion.xo_ref), channel_id=1, source_target_pairs={{0,1},{1,0},{2,3},{3,2},{4,5},{5,4},{6,7},{7,6},{8,9},{9,8},{10,11... | collective-permute-start | bytes 4423688 | tf_op jit(solution)/shard_map/ppermute | solution.py:27
  56.3 18.1 %collective-permute-start.17 = (bf16[2,184,256]{2,1,0:T(8,128)(2,1)S(1)}, bf16[2,184,256]{2,1,0:T(8,128)(2,1)S(1)}, u32[]{:S(2)}, u32[]{:S(2)}) collective-permute-start(bf16[2,184,256]{2,1,0:T(8,128)(2,1)S(1)} %slice.109), channel_id=1, source_target_pairs={{0,8},{8,16},{16,24},{24,0},{1,9},{9,17},{17,25},{25,1},{2,10},{10... | collective-permute-start | bytes 565256 | tf_op jit(solution)/shard_map/ppermute | solution.py:23
  56.4 18.0 %collective-permute-start.18 = (bf16[2,184,256]{2,1,0:T(8,128)(2,1)S(1)}, bf16[2,184,256]{2,1,0:T(8,128)(2,1)S(1)}, u32[]{:S(2)}, u32[]{:S(2)}) collective-permute-start(bf16[2,184,256]{2,1,0:T(8,128)(2,1)S(1)} %slice.110), channel_id=1, source_target_pairs={{0,24},{8,0},{16,8},{24,16},{1,25},{9,1},{17,9},{25,17},{2,26},{10... | collective-permute-start | bytes 565256 | tf_op jit(solution)/shard_map/ppermute | solution.py:23
  59.1 10.1 %collective-permute-start.19 = (bf16[2,184,384]{2,1,0:T(8,128)(2,1)S(1)}, bf16[2,184,384]{2,1,0:T(8,128)(2,1)S(1)}, u32[]{:S(2)}, u32[]{:S(2)}) collective-permute-start(bf16[2,184,384]{2,1,0:T(8,128)(2,1)S(1)} %slice.111), channel_id=1, source_target_pairs={{0,32},{32,64},{64,96},{96,0},{1,33},{33,65},{65,97},{97,1},{2,34}... | collective-permute-start | bytes 847880 | tf_op jit(solution)/shard_map/ppermute | solution.py:23
  59.3 9.9 %collective-permute-start.20 = (bf16[2,184,384]{2,1,0:T(8,128)(2,1)S(1)}, bf16[2,184,384]{2,1,0:T(8,128)(2,1)S(1)}, u32[]{:S(2)}, u32[]{:S(2)}) collective-permute-start(bf16[2,184,384]{2,1,0:T(8,128)(2,1)S(1)} %slice.112), channel_id=1, source_target_pairs={{0,96},{32,0},{64,32},{96,64},{1,97},{33,1},{65,33},{97,65},{2,98}... | collective-permute-start | bytes 847880 | tf_op jit(solution)/shard_map/ppermute | solution.py:23
  73.1 9.2 %collective-permute-start.21 = (bf16[128,128]{1,0:T(8,128)(2,1)S(1)}, bf16[128,128]{1,0:T(8,128)(2,1)S(1)}, u32[]{:S(2)}, u32[]{:S(2)}) collective-permute-start(bf16[128,128]{1,0:T(8,128)(2,1)S(1)} %slice.113), channel_id=1, source_target_pairs={{0,8},{8,16},{16,24},{24,32},{32,40},{40,48},{48,56},{56,64},{64,7... | collective-permute-start | bytes 98312 | tf_op jit(solution)/shard_map/ppermute | solution.py:370
  96.7 6.0 %collective-permute-start.25 = (bf16[32,2880]{1,0:T(8,128)(2,1)S(1)}, bf16[32,2880]{1,0:T(8,128)(2,1)S(1)}, u32[]{:S(2)}, u32[]{:S(2)}) collective-permute-start(bf16[32,2880]{1,0:T(8,128)(2,1)S(1)} %get-tuple-element.25), channel_id=1, source_target_pairs={{0,6},{2,0},{4,2},{6,4},{1,7},{3,1},{5,3},{7,5},{8,14},{10,8},{12,... | collective-permute-start | bytes 552968 | tf_op jit(solution)/shard_map/ppermute | solution.py:23
  98.1 7.3 %collective-permute-start.23 = (bf16[32,2880]{1,0:T(8,128)(2,1)S(1)}, bf16[32,2880]{1,0:T(8,128)(2,1)S(1)}, u32[]{:S(2)}, u32[]{:S(2)}) collective-permute-start(bf16[32,2880]{1,0:T(8,128)(2,1)S(1)} %get-tuple-element.23), channel_id=1, source_target_pairs={{0,2},{2,4},{4,6},{6,0},{1,3},{3,5},{5,7},{7,1},{8,10},{10,12},{12... | collective-permute-start | bytes 552968 | tf_op jit(solution)/shard_map/ppermute | solution.py:23
  102.8 9.4 %collective-permute-start.26 = (bf16[64,2880]{1,0:T(8,128)(2,1)S(1)}, bf16[64,2880]{1,0:T(8,128)(2,1)S(1)}, u32[]{:S(2)}, u32[]{:S(2)}) collective-permute-start(bf16[64,2880]{1,0:T(8,128)(2,1)S(1)} %pad_maximum_fusion.4), channel_id=1, source_target_pairs={{0,6},{2,0},{4,2},{6,4},{1,7},{3,1},{5,3},{7,5},{8,14},{10,8},{12,... | collective-permute-start | bytes 1105928 | tf_op jit(solution)/shard_map/ppermute | solution.py:23
  105.4 10.1 %collective-permute-start.24 = (bf16[64,2880]{1,0:T(8,128)(2,1)S(1)}, bf16[64,2880]{1,0:T(8,128)(2,1)S(1)}, u32[]{:S(2)}, u32[]{:S(2)}) collective-permute-start(bf16[64,2880]{1,0:T(8,128)(2,1)S(1)} %pad_maximum_fusion.3), channel_id=1, source_target_pairs={{0,2},{2,4},{4,6},{6,0},{1,3},{3,5},{5,7},{7,1},{8,10},{10,12},{12... | collective-permute-start | bytes 1105928 | tf_op jit(solution)/shard_map/ppermute | solution.py:23
  (15 other events, 100.8 us)
Sparse Core Ops, SparseCore 0:
  10.2 51.4 all-gather.2

commit v2 on v1

v2 whole, which is shorter than its diff:
```python
import functools

import jax
import jax.numpy as jnp
from jax import lax
from jax.experimental import pallas as pl
from jax.experimental.pallas import tpu as pltpu
from jax.sharding import Mesh
from jax.sharding import PartitionSpec as P

WINDOW = 128
ROPE_BASE = 150000.0
BF = jnp.bfloat16
F32 = jnp.float32
LOG2E = 1.4426950408889634
OFFSETS = (0, -1, 1, 2)
VMEM = pl.BlockSpec(memory_space=pltpu.VMEM)
SMEM = pl.BlockSpec(memory_space=pltpu.SMEM)


def shifted(block, axis, distance):
    return lax.ppermute(block, axis, [(i, (i + distance) % 4) for i in range(4)])


def swapped(block):
    return lax.ppermute(block, "c", [(0, 1), (1, 0)])


def after(value, *others):
    return lax.optimization_barrier((value, *others))[0]


def near(block, axis):
    return shifted(block, axis, 1), shifted(block, axis, -1)


def passed_on(pair, axis):
    return shifted(pair[0][:2], axis, 1), shifted(pair[1][2:], axis, -1)


def rms_norm(values, gain):
    wide = values.astype(F32)
    scale = lax.rsqrt(jnp.mean(wide * wide, axis=-1, keepdims=True) + 1e-05)
    return (wide * scale * gain).astype(BF)


def params(limit):
    return pltpu.CompilerParams(vmem_limit_bytes=limit << 20)


def cost(flops, moved):
    return pl.CostEstimate(flops=flops, bytes_accessed=moved, transcendentals=0)


def shard_of(at_ref, first, second, first_is_x):
    dx, dz = (first, second) if first_is_x else (second, first)
    x = lax.rem(at_ref[0] + (OFFSETS[dx] + 4), 4)
    z = lax.rem(at_ref[1] + (OFFSETS[dz] + 4), 4)
    return x * 4 + z


def rotated(values, cos, sin):
    lanes = values.shape[1]
    lane = lax.broadcasted_iota(jnp.int32, values.shape, 1)
    low = lax.rem(lane, 64) < 32
    other = jnp.where(low, pltpu.roll(values, lanes - 32, 1), pltpu.roll(values, 32, 1))
    return values * cos + other * sin


def row_starts(at_ref):
    for core in range(2):
        for offset in OFFSETS:
            y = lax.rem(at_ref[2] + (offset + 4), 4)
            c = at_ref[3] if core == 0 else 1 - at_ref[3]
            yield pl.multiple_of((y * 2 + c) * 64, 64)


def in_order(at_ref, ref):
    return jnp.concatenate([ref[pl.ds(start, 64), :] for start in row_starts(at_ref)], 0)


def projection_kernel(at_ref, cos_ref, sin_ref, xo_ref, xs_ref, *refs):
    a_refs, b_refs, (q_ref, kv_ref, x_ref, w_ref) = refs[:5], refs[5:10], refs[10:]
    depth = a_refs[0].shape[1]
    for half, group in enumerate((a_refs, b_refs)):
        for first in range(4):
            for second in range(4):
                ref, index = (group[first], second) if first < 3 else (group[3 + second // 2], second % 2)
                start = shard_of(at_ref, first, second, half == 1) * (2 * depth) + half * depth
                w_ref[pl.ds(pl.multiple_of(start, depth), depth), :] = ref[index]
    for core, ref in enumerate((xo_ref, xs_ref)):
        for i in range(4):
            x_ref[core * 256 + i * 64 : core * 256 + i * 64 + 64] = ref[i]
    total = jnp.dot(x_ref[...], w_ref[...], preferred_element_type=F32)
    cos, sin = in_order(at_ref, cos_ref), in_order(at_ref, sin_ref)
    lane = lax.broadcasted_iota(jnp.int32, cos.shape, 1)
    for column in range(0, 640, 128):
        part = total[:, column : column + 128]
        turned = rotated(part, cos, sin)
        if column == 512:
            turned = jnp.where(lane < 64, turned, part)
        turned = turned.astype(BF)
        for i, start in enumerate(row_starts(at_ref)):
            rows = turned[i * 64 : i * 64 + 64]
            if column == 512:
                kv_ref[pl.ds(start, 64), :] = rows
            else:
                q_ref[pl.ds(start, 64), column : column + 128] = rows


def attended_heads(query, both, allowed, sinks_ref):
    pair = lax.broadcasted_iota(jnp.int32, (4 * WINDOW, 1), 0) // WINDOW
    zero = jnp.zeros((2 * WINDOW, 64), BF)
    key, value = both[:, :64], both[:, 64:]
    keys = jnp.concatenate([jnp.concatenate([key, zero], 1), jnp.concatenate([zero, key], 1)], 0)
    values = jnp.concatenate(
        [jnp.concatenate([value, zero], 1), jnp.concatenate([zero, value], 1)], 0
    )
    query = jnp.concatenate([query[:, p * 128 : (p + 1) * 128] for p in range(4)], 0)
    scores = lax.dot_general(query, keys, (((1,), (1,)), ((), ())), preferred_element_type=F32)
    probs = []
    for odd in range(2):
        level = jnp.zeros((4 * WINDOW, 1), F32)
        for p in range(4):
            level = jnp.where(pair == p, sinks_ref[0, 2 * p + odd], level)
        part = scores[:, odd * 256 : odd * 256 + 256]
        expo = jnp.where(allowed, jnp.exp2(part * (0.125 * LOG2E) - 20.0), 0.0)
        denom = jnp.sum(expo, axis=1, keepdims=True) + jnp.exp2(level * LOG2E - 20.0)
        probs.append((expo * (1.0 / denom)).astype(BF))
    out = jnp.dot(jnp.concatenate(probs, 1), values, preferred_element_type=F32).astype(BF)
    return jnp.concatenate([out[p * WINDOW : (p + 1) * WINDOW] for p in range(4)], 1)


def window_mask():
    shape = (4 * WINDOW, 2 * WINDOW)
    row = lax.rem(lax.broadcasted_iota(jnp.int32, shape, 0), WINDOW)
    column = lax.broadcasted_iota(jnp.int32, shape, 1)
    return (column > row) & (column <= row + WINDOW), column


def later_kernel(q_ref, kv_ref, sinks_ref, out_ref):
    allowed, _ = window_mask()
    for i in range(1, q_ref.shape[0] // WINDOW):
        rows = slice(i * WINDOW, (i + 1) * WINDOW)
        out_ref[(i - 1) * WINDOW : i * WINDOW] = attended_heads(
            q_ref[rows], kv_ref[(i - 1) * WINDOW : (i + 1) * WINDOW], allowed, sinks_ref
        )


def first_kernel(at_ref, q_ref, kv_ref, before_ref, later_ref, sinks_ref, out_ref):
    allowed, column = window_mask()
    is_first = (at_ref[0] == 0) & (at_ref[1] == 0)
    allowed = allowed & ((column >= WINDOW) | jnp.logical_not(is_first))
    both = jnp.concatenate([before_ref[...], kv_ref[...]], 0)
    out_ref[:WINDOW] = attended_heads(q_ref[...], both, allowed, sinks_ref)
    out_ref[WINDOW:] = later_ref[...]


def head_rows(at_ref, heads_ref, is_other):
    c = 1 - at_ref[3] if is_other else at_ref[3]
    rows = []
    for step in range(4):
        start = (lax.rem(at_ref[2] + step, 4) * 2 + c) * 64
        rows.append(heads_ref[pl.ds(pl.multiple_of(start, 64), 64), :])
    return jnp.concatenate(rows, 0)


def other_kernel(at_ref, heads_ref, w_ref, out_ref):
    rows = head_rows(at_ref, heads_ref, True)
    total = jnp.dot(rows, w_ref[...], preferred_element_type=F32).astype(BF)
    for i in range(4):
        out_ref[i] = total[i * 64 : i * 64 + 64]


def own_kernel(at_ref, heads_ref, w_ref, got_ref, up_ref, down_ref, one_ref, three_ref, zero_ref):
    rows = head_rows(at_ref, heads_ref, False)
    total = jnp.dot(rows, w_ref[...], preferred_element_type=F32)
    block = lambda i: total[i * 64 : i * 64 + 64] + got_ref[i].astype(F32)
    far_block = block(2).astype(BF)
    up_ref[...] = far_block[:32]
    down_ref[...] = far_block[32:]
    one_ref[...] = block(1)
    three_ref[...] = block(3)
    zero_ref[...] = block(0)


def dispatch_kernel(place_ref, own_ref, other_ref, out_ref):
    rows = jnp.concatenate([own_ref[...], other_ref[...]], 0)
    out_ref[...] = jnp.dot(place_ref[...], rows, preferred_element_type=F32).astype(BF)


def combine_kernel(weights_ref, rows_ref, own_ref, other_ref):
    both = jnp.dot(weights_ref[...], rows_ref[...], preferred_element_type=F32)
    total = both[:128] + both[128:]
    own_ref[...] = total[:64]
    other_ref[...] = total[64:].astype(BF)


TILE = 512


def activate(both_ref, act_ref, first, last, width):
    for start in range(0, both_ref.shape[0], 64):
        rows = slice(start, start + 64)
        gate = both_ref[rows, first:last]
        upper = both_ref[rows, width + first : width + last]
        act_ref[rows, first:last] = ((upper + 1.0) * gate * jax.nn.sigmoid(1.702 * gate)).astype(BF)


def expert_kernel(steps, width, rows_ref, gu_ref, down_ref, out_ref, both_ref, act_ref):
    step = pl.program_id(0)
    ready = {}
    for first in range(0, width, TILE):
        last = min(first + TILE, width)
        ready.setdefault((width + last - 1) // TILE + 1, []).append((first, last))

    for i in range(steps):

        @pl.when(step == i)
        def _():
            both_ref[:, i * TILE : (i + 1) * TILE] = jnp.dot(
                rows_ref[...], gu_ref[0], preferred_element_type=F32
            )
            for first, last in ready.get(i, ()):
                activate(both_ref, act_ref, first, last, width)

    @pl.when(step == steps)
    def _():
        for first, last in ready.get(steps, ()):
            activate(both_ref, act_ref, first, last, width)

    @pl.when(step >= steps)
    def _():
        out_ref[...] = jnp.dot(act_ref[...], down_ref[0], preferred_element_type=F32).astype(BF)


def expert_ffn(rows, gate_up, down):
    count, model = rows.shape
    width = down.shape[1]
    steps = pl.cdiv(2 * width, TILE)
    return pl.pallas_call(
        functools.partial(expert_kernel, steps, width),
        grid=(steps + pl.cdiv(model, TILE),),
        out_shape=jax.ShapeDtypeStruct((count, model), BF),
        in_specs=[
            pl.BlockSpec((count, model), lambda i: (0, 0)),
            pl.BlockSpec((1, model, TILE), lambda i: (0, 0, jnp.minimum(i, steps - 1))),
            pl.BlockSpec((1, width, TILE), lambda i: (0, 0, jnp.maximum(i - steps, 0))),
        ],
        out_specs=pl.BlockSpec((count, TILE), lambda i: (0, jnp.maximum(i - steps, 0))),
        scratch_shapes=[
            pltpu.VMEM((count, steps * TILE), F32),
            pltpu.VMEM((count, width), BF),
        ],
        compiler_params=params(56),
        cost_estimate=cost(2 * count * model * 3 * width, 31_000_000),
        name="experts",
    )(rows, gate_up, down)


def routing(ids, weights, core, slots, experts):
    count = ids.shape[1]
    total = experts // 2 * 2 * slots
    slot = jnp.arange(total, dtype=jnp.int32)[:, None]
    expert = slot // (2 * slots) * 2 + core
    token = jnp.arange(count, dtype=jnp.int32)
    named = jnp.zeros((total, count), F32)
    weight = jnp.zeros((total, count), F32)
    for j in range(ids.shape[0]):
        same = ids[j][None, :] == expert
        named = named + same.astype(F32)
        weight = weight + jnp.where(same, weights[j][None, :], 0.0)
    half = count // 2
    earlier = (token[:, None] < token[None, :]) & (token[:, None] // half == token[None, :] // half)
    rank = jnp.dot(named.astype(BF), earlier.astype(BF), preferred_element_type=F32)
    here = (rank == (slot % slots).astype(F32)) & (slot // slots % 2 == token[None, :] // half)
    place = jnp.where(here, named, 0.0).astype(BF)
    weighted = jnp.where(here, weight, 0.0).T
    high = lax.reduce_precision(weighted, 8, 7)
    return place, jnp.concatenate([high, weighted - high], 0).astype(BF)


def on_device(
    tokens, attn_gain, moe_gain, q_weight, kv_weight, o_weight, sinks, gate_up, down, expert_ids, route_weights
):
    rows, width = tokens.shape
    barrier = lax.optimization_barrier
    at = jnp.stack([lax.axis_index(a) for a in ("x", "z", "y", "c")]).astype(jnp.int32)

    normed = rms_norm(tokens, attn_gain)
    o_all = lax.all_gather(o_weight[:, 0, :], ("x", "z"), axis=0, tiled=True)
    span = 8 * rows

    shard, depth = q_weight.shape[0], 96
    joined = jnp.concatenate([q_weight[:, 0, :], kv_weight[:, 0, :]], axis=1)
    joined = jnp.pad(joined, ((0, 2 * depth - shard), (0, 0)))
    a, b = joined[:depth], joined[depth:]
    a_near, b_near = near(a, "x"), near(b, "z")
    spread = jnp.pad(normed.reshape(rows, 16, shard), ((0, 0), (0, 0), (0, 2 * depth - shard)))
    spread = spread.reshape(rows, 32 * depth)
    x_fore = shifted(spread, "y", 1)
    a_far = shifted(after(a, *a_near, *b_near), "x", 2)
    b_far = shifted(after(b, *a_near, *b_near), "z", 2)
    x_back = shifted(after(spread, *a_near, *b_near), "y", -1)
    a_stack, b_stack = jnp.stack((a, *a_near, a_far)), jnp.stack((b, *b_near, b_far))
    a_stack, b_stack, _ = barrier((a_stack, b_stack, x_fore))
    x_far = shifted(after(spread, a_stack, b_stack, x_back), "y", 2)
    a_near, b_near = near(a_stack, "z"), near(b_stack, "x")
    *x_parts, a_fore, a_back, b_fore, b_back = barrier(
        (spread, x_fore, x_back, x_far, *a_near, *b_near)
    )
    a_near, b_near = (a_fore, a_back), (b_fore, b_back)
    x_own = jnp.stack(x_parts)
    x_other = swapped(x_own)
    mine = jnp.concatenate([expert_ids.astype(F32), route_weights], axis=1)
    theirs = swapped(after(mine, a_stack, b_stack))
    a_parts = (a_stack, *a_near, *passed_on(a_near, "z"))
    b_parts = (b_stack, *b_near, *passed_on(b_near, "x"))

    half = 32
    freq = ROPE_BASE ** (-(jnp.arange(half, dtype=F32) * 2.0) / (2.0 * half))
    first = (at[0] * 4 + at[1]) * span
    angle = (first + jnp.arange(span, dtype=jnp.int32)).astype(F32)[:, None] * freq
    cos, sin = jnp.cos(angle), jnp.sin(angle)
    cos = jnp.concatenate([cos] * 4, axis=1)
    sin = jnp.concatenate([-sin, sin, -sin, sin], axis=1)

    table = jnp.concatenate([mine, theirs], axis=0).T
    topk = expert_ids.shape[1]
    place, weighted = routing(table[:topk].astype(jnp.int32), table[topk:], at[3], 4, 128)
    at, place, weighted = barrier((at, place, weighted))

    query, kv = pl.pallas_call(
        projection_kernel,
        out_shape=[jax.ShapeDtypeStruct((span, n), BF) for n in (512, 128)],
        in_specs=[SMEM] + [VMEM] * 14,
        out_specs=[VMEM] * 2,
        scratch_shapes=[
            pltpu.VMEM((span, 32 * depth), BF),
            pltpu.VMEM((32 * depth, 640), BF),
        ],
        compiler_params=params(20),
        cost_estimate=cost(2 * span * width * 640, 12_000_000),
        name="projection",
    )(at, cos, sin, x_own, x_other, *a_parts, *b_parts)
    before = lax.ppermute(kv[span - WINDOW :], ("x", "z"), [(i, i + 1) for i in range(15)])
    later = pl.pallas_call(
        later_kernel,
        out_shape=jax.ShapeDtypeStruct((span - WINDOW, 512), BF),
        in_specs=[VMEM] * 2 + [SMEM],
        out_specs=VMEM,
        compiler_params=params(12),
        cost_estimate=cost(3_000_000_000, 2_000_000),
        name="later",
    )(query, kv, sinks)
    before, o_all = barrier((before, o_all))
    heads = pl.pallas_call(
        first_kernel,
        out_shape=jax.ShapeDtypeStruct((span, 512), BF),
        in_specs=[SMEM] + [VMEM] * 4 + [SMEM],
        out_specs=VMEM,
        compiler_params=params(12),
        cost_estimate=cost(1_000_000_000, 1_000_000),
        name="first",
    )(at, query[:WINDOW], kv[:WINDOW], before, later, sinks)

    shape = lambda dtype, *dims: jax.ShapeDtypeStruct((*dims, width), dtype)
    other = pl.pallas_call(
        other_kernel,
        out_shape=shape(BF, 4, rows),
        in_specs=[SMEM] + [VMEM] * 2,
        out_specs=VMEM,
        compiler_params=params(12),
        cost_estimate=cost(span * width * 512, 5_000_000),
        name="other",
    )(at, heads, o_all)
    up, down_, one, three, zero = pl.pallas_call(
        own_kernel,
        out_shape=[shape(BF, 32)] * 2 + [shape(F32, rows)] * 3,
        in_specs=[SMEM] + [VMEM] * 3,
        out_specs=[VMEM] * 5,
        compiler_params=params(12),
        cost_estimate=cost(span * width * 512, 8_000_000),
        name="own",
    )(at, heads, o_all, swapped(other))
    wide = lambda array: array.astype(F32)
    up, down_ = shifted(up, "y", 1), shifted(down_, "y", -1)
    ahead = jnp.concatenate([one[:32] + wide(up), one[32:]]).astype(BF)
    behind = jnp.concatenate([three[:32], three[32:] + wide(down_)]).astype(BF)
    left, right = shifted(ahead, "y", 1), shifted(behind, "y", -1)
    attended = (wide(tokens) + (zero + wide(left) + wide(right))).astype(BF)
    moe_in = rms_norm(attended, moe_gain)

    slots = place.shape[0]
    outgoing = pl.pallas_call(
        dispatch_kernel,
        out_shape=jax.ShapeDtypeStruct((slots, width), BF),
        in_specs=[VMEM] * 3,
        out_specs=VMEM,
        compiler_params=params(12),
        name="dispatch",
    )(place, moe_in, swapped(moe_in))
    exchange = lambda array: lax.all_to_all(
        array.reshape(64, 8, width), ("x", "z", "y"), split_axis=0, concat_axis=0, tiled=True
    ).reshape(slots, width)
    result = expert_ffn(exchange(outgoing), gate_up, down)
    mine_out, their_out = pl.pallas_call(
        combine_kernel,
        out_shape=[jax.ShapeDtypeStruct((rows, width), dtype) for dtype in (F32, BF)],
        in_specs=[VMEM] * 2,
        out_specs=[VMEM] * 2,
        compiler_params=params(12),
        name="combine",
    )(weighted, exchange(result))
    return attended, (mine_out + wide(swapped(their_out))).astype(BF)


def solution(mesh):
    fine = Mesh(mesh.devices.reshape(4, 4, 4, 2), ("x", "z", "y", "c"))
    seq, tp, every = ("x", "z"), ("y", "c"), ("x", "z", "y", "c")
    placed = (
        P(every, None),
        P(),
        P(),
        P(seq, tp, None),
        P(seq, tp, None),
        P(seq, tp, None),
        P(tp, None),
        P(every, None, None),
        P(every, None, None),
        P(every, None),
        P(every, None),
    )
    return jax.shard_map(
        on_device,
        mesh=fine,
        in_specs=placed,
        out_specs=(P(every, None), P(every, None)),
        check_vma=False,
    )
```

time: 250 us -> 238 us (0.952)
  Pallas kernels: 45.6 us -> 35.6 us
    pallas_call x5, Pallas kernels: 20 us -> 10.1 us  [the longest x1 3.9 us: on_device(): pl.pallas_call(projection_kernel, out_shape=[jax.ShapeDtypeStruct((span,...]
    ppermute x23 -> x21, waiting for transfers between devices: 30.2 us -> 27.1 us  [shifted(): lax.ppermute(block, axis, [(i, (i + distance) % 4) for i in range(4)])]
    ppermute x23 -> x21, starting transfers between devices: 34.2 us -> 32 us  [shifted(): lax.ppermute(block, axis, [(i, (i + distance) % 4) for i in range(4)])]
  transfers between devices with their start and end apart: 30 -> 28, of which waited for: 11 -> 13; matrix products, arithmetic and copies ran while one was open for 3% -> 4% of each run, Pallas kernels for 6% -> 2%
where the time goes in v2:
time: 238 us; the launch traced here: 237 us
  blocking collectives  91.9 us (39%)
  starting transfers between devices  48.1 us (20%)
  waiting for transfers between devices  36.2 us (15%)
  Pallas kernels  35.6 us (15%)
  between operations  14.4 us (6%)
  other arithmetic  7.43 us (3%)
  local copies, waits for them, and re-layouts  3.15 us (1%)
    all_to_all x2, blocking collectives, on_device(): lax.all_to_all(array.reshape(64, 8, width), ('x', 'z', 'y'), split_axis=0...  91.9 us
    ppermute x21, starting transfers between devices, shifted(): lax.ppermute(block, axis, [(i, (i + distance) % 4) for i in range(4)])  32 us
    ppermute x21, waiting for transfers between devices, shifted(): lax.ppermute(block, axis, [(i, (i + distance) % 4) for i in range(4)])  27.1 us
    pallas_call x1, Pallas kernels, expert_ffn(): pl.pallas_call(functools.partial(expert_kernel, steps, width), grid=(step...  23.6 us
    ppermute x5, starting transfers between devices, swapped(): return lax.ppermute(block, 'c', [(0, 1), (1, 0)])  14.8 us
    ppermute x5, waiting for transfers between devices, swapped(): return lax.ppermute(block, 'c', [(0, 1), (1, 0)])  8.34 us
  transfers between devices with their start and end apart: 28, of which 13 were waited for; matrix products, arithmetic and copies ran while one was open for 4% of the time, Pallas kernels for 2%

profile of v2, /device:TPU:1, one launch (start us, length us, event | category | flops | bytes accessed | tf_op | source)
XLA Modules:
  0.0 237.3 jit_solution(8224018317943138233)
XLA Ops:
  8.8 2.1 collective-permute-start
  15.1 2.2 collective-permute-start.3
  24.5 2.3 collective-permute-start.5
  26.9 3.3 %collective-permute-done.5 = bf16[96,640]{1,0:T(8,128)(2,1)S(1)} collective-permute-done((bf16[96,640]{1,0:T(8,128)(2,1)S(1)}, bf16[96,640]{1,0:T(8,128)(2,1)S(1)}, u32[]{:S(2)}, u32[]{:S(2)}) %collective-permute-start.5) | collective-permute-done | bytes 122912 | tf_op jit(solution)/shard_map/ppermute | solution.py:22
  31.1 2.1 collective-permute-start.11
  33.9 2.0 collective-permute-start.13
  35.9 2.3 collective-permute-start.9
  39.7 3.7 %collective-permute-done.10.refs_1_ = bf16[4,96,640]{2,1,0:T(8,128)(2,1)S(1)} collective-permute-done((bf16[4,96,640]{2,1,0:T(8,128)(2,1)S(1)}, bf16[4,96,640]{2,1,0:T(8,128)(2,1)S(1)}, u32[]{:S(2)}, u32[]{:S(2)}) %collective-permute-start.10) | collective-permute-done | bytes 491552 | tf_op jit(solution)/shard_map/ppermute | solution.py:22
  45.8 7.5 %collective-permute-start.14 = (bf16[4,64,3072]{2,1,0:T(8,128)(2,1)S(1)}, bf16[4,64,3072]{2,1,0:T(8,128)(2,1)S(1)}, u32[]{:S(2)}, u32[]{:S(2)}) collective-permute-start(bf16[4,64,3072]{2,1,0:T(8,128)(2,1)S(1)} %pad_maximum_fusion.xo_ref), channel_id=1, source_target_pairs={{0,1},{1,0},{2,3},{3,2},{4,5},{5,4},{6,7},{7,6},{8,9},{9,8},{10,11... | collective-permute-start | bytes 4718600 | tf_op jit(solution)/shard_map/ppermute | solution.py:26
  53.5 2.9 %collective-permute-done.7 = f32[64,8]{0,1:T(8,128)S(1)} collective-permute-done((f32[64,8]{0,1:T(8,128)S(1)}, f32[64,8]{0,1:T(8,128)S(1)}, u32[]{:S(2)}, u32[]{:S(2)}) %collective-permute-start.7) | collective-permute-done | bytes 2080 | tf_op jit(solution)/shard_map/ppermute | solution.py:26
  57.0 2.7 %collective-permute-start.16 = (bf16[2,96,640]{2,1,0:T(8,128)(2,1)S(1)}, bf16[2,96,640]{2,1,0:T(8,128)(2,1)S(1)}, u32[]{:S(2)}, u32[]{:S(2)}) collective-permute-start(bf16[2,96,640]{2,1,0:T(8,128)(2,1)S(1)} %slice.86), channel_id=1, source_target_pairs={{0,24},{8,0},{16,8},{24,16},{1,25},{9,1},{17,9},{25,17},{2,26},{10... | collective-permute-start | bytes 737288 | tf_op jit(solution)/shard_map/ppermute | solution.py:22
  59.9 3.7 %collective-permute-start.18 = (bf16[2,96,640]{2,1,0:T(8,128)(2,1)S(1)}, bf16[2,96,640]{2,1,0:T(8,128)(2,1)S(1)}, u32[]{:S(2)}, u32[]{:S(2)}) collective-permute-start(bf16[2,96,640]{2,1,0:T(8,128)(2,1)S(1)} %slice.88), channel_id=1, source_target_pairs={{0,96},{32,0},{64,32},{96,64},{1,97},{33,1},{65,33},{97,65},{2,98}... | collective-permute-start | bytes 737288 | tf_op jit(solution)/shard_map/ppermute | solution.py:22
  65.3 3.3 %collective-permute-done.17.refs_8_ = bf16[2,96,640]{2,1,0:T(8,128)(2,1)S(1)} collective-permute-done((bf16[2,96,640]{2,1,0:T(8,128)(2,1)S(1)}, bf16[2,96,640]{2,1,0:T(8,128)(2,1)S(1)}, u32[]{:S(2)}, u32[]{:S(2)}) %collective-permute-start.17) | collective-permute-done | bytes 245792 | tf_op jit(solution)/shard_map/ppermute | solution.py:22
  68.6 3.9 %projection.1 = (bf16[512,512]{1,0:T(8,128)(2,1)S(1)}, bf16[512,128]{1,0:T(8,128)(2,1)S(1)}) custom-call(s32[4]{0:T(128)S(1)} %pad_add_fusion.at_ref, f32[512,128]{1,0:T(8,128)S(1)} %get-tuple-element.83.cos_ref, f32[512,128]{1,0:T(8,128)S(1)} %get-tuple-element.84.sin_ref, bf16[4,64,3072]{2,1,0:T(8,128)(2,1)S(1)} %pad_maximum_fusion.xo_ref, ...), custom_call_target="tpu_custom_call" | custom-call | flops 1887436800 | bytes 12000000 | tf_op jit(solution)/shard_map/projection/pallas_call | solution.py:333
  73.9 1.9 later.1.later_ref
  80.8 2.9 %collective-permute-done.20.got_ref = bf16[4,64,2880]{2,1,0:T(8,128)(2,1)S(1)} collective-permute-done((bf16[4,64,2880]{2,1,0:T(8,128)(2,1)S(1)}, bf16[4,64,2880]{2,1,0:T(8,128)(2,1)S(1)}, u32[]{:S(2)}, u32[]{:S(2)}) %collective-permute-start.20) | collective-permute-done | bytes 1474592 | tf_op jit(solution)/shard_map/ppermute | solution.py:26
  87.0 4.3 %collective-permute-done.23 = bf16[32,2880]{1,0:T(8,128)(2,1)S(1)} collective-permute-done((bf16[32,2880]{1,0:T(8,128)(2,1)S(1)}, bf16[32,2880]{1,0:T(8,128)(2,1)S(1)}, u32[]{:S(2)}, u32[]{:S(2)}) %collective-permute-start.23) | collective-permute-done | bytes 184352 | tf_op jit(solution)/shard_map/ppermute | solution.py:22
  93.4 7.1 %collective-permute-done.24 = bf16[64,2880]{1,0:T(8,128)(2,1)S(1)} collective-permute-done((bf16[64,2880]{1,0:T(8,128)(2,1)S(1)}, bf16[64,2880]{1,0:T(8,128)(2,1)S(1)}, u32[]{:S(2)}, u32[]{:S(2)}) %collective-permute-start.24) | collective-permute-done | bytes 368672 | tf_op jit(solution)/shard_map/ppermute | solution.py:22
  100.5 2.8 %collective-permute-done.22 = bf16[64,2880]{1,0:T(8,128)(2,1)S(1)} collective-permute-done((bf16[64,2880]{1,0:T(8,128)(2,1)S(1)}, bf16[64,2880]{1,0:T(8,128)(2,1)S(1)}, u32[]{:S(2)}, u32[]{:S(2)}) %collective-permute-start.22) | collective-permute-done | bytes 368672 | tf_op jit(solution)/shard_map/ppermute | solution.py:22
  103.9 2.5 %collective-permute-start.25 = (bf16[64,2880]{1,0:T(8,128)(2,1)S(1)}, bf16[64,2880]{1,0:T(8,128)(2,1)S(1)}, u32[]{:S(2)}, u32[]{:S(2)}) collective-permute-start(bf16[64,2880]{1,0:T(8,128)(2,1)S(1)} %fusion.2.own_ref), channel_id=1, source_target_pairs={{0,1},{1,0},{2,3},{3,2},{4,5},{5,4},{6,7},{7,6},{8,9},{9,8},{10,11... | collective-permute-start | bytes 1105928 | tf_op jit(solution)/shard_map/ppermute | solution.py:26
  108.7 47.5 %all_to_all.10 = bf16[64,8,2880]{2,1,0:T(8,128)(2,1)} all-to-all(bf16[64,8,2880]{2,1,0:T(8,128)(2,1)S(1)} %bitcast.51), channel_id=1, replica_groups=mesh['x'=4,'z'=4,'y'=4,'c'=2] {'x','z','y'}, dimensions={0} | all-to-all | bytes 5898240 | tf_op jit(solution)/shard_map/all_to_all | solution.py:403
  156.2 23.6 %experts.1 = bf16[512,2880]{1,0:T(8,128)(2,1)} custom-call(bf16[512,2880]{1,0:T(8,128)(2,1)} %bitcast.54, bf16[1,2880,2880]{2,1,0:T(8,128)(2,1)} %gu_ref.1, bf16[1,1440,2880]{2,1,0:T(8,128)(2,1)} %down_ref.1), custom_call_target="tpu_custom_call" | custom-call | flops 12740198400 | bytes 31000000 | tf_op jit(solution)/shard_map/experts/pallas_call | solution.py:241
  179.8 44.4 %all_to_all.11 = bf16[64,8,2880]{2,1,0:T(8,128)(2,1)S(1)} all-to-all(bf16[64,8,2880]{2,1,0:T(8,128)(2,1)} %bitcast.55), channel_id=1, replica_groups=mesh['x'=4,'z'=4,'y'=4,'c'=2] {'x','z','y'}, dimensions={0} | all-to-all | bytes 5898240 | tf_op jit(solution)/shard_map/all_to_all | solution.py:403
  225.2 3.1 %collective-permute-start.26 = (bf16[64,2880]{1,0:T(8,128)(2,1)S(1)}, bf16[64,2880]{1,0:T(8,128)(2,1)S(1)}, u32[]{:S(2)}, u32[]{:S(2)}) collective-permute-start(bf16[64,2880]{1,0:T(8,128)(2,1)S(1)} %get-tuple-element.59), channel_id=1, source_target_pairs={{0,1},{1,0},{2,3},{3,2},{4,5},{5,4},{6,7},{7,6},{8,9},{9,8},{10,11... | collective-permute-start | bytes 1105928 | tf_op jit(solution)/shard_map/ppermute | solution.py:26
  (107 shorter events, 38.6 us)
Async XLA Ops:
  7.2 68.6 %all-gather.3.cloned.1.call-start = ((), (), s32[]{:S(2)}) async-start(), calls=%async_computation.2 | async-start | bytes 3203072 | tf_op jit(solution)/shard_map/all_gather | solution.py:291
  8.8 12.4 %collective-permute-start = (bf16[96,640]{1,0:T(8,128)(2,1)S(1)}, bf16[96,640]{1,0:T(8,128)(2,1)S(1)}, u32[]{:S(2)}, u32[]{:S(2)}) collective-permute-start(bf16[96,640]{1,0:T(8,128)(2,1)S(1)} %fusion.15), channel_id=1, source_target_pairs={{0,32},{32,64},{64,96},{96,0},{1,33},{33,65},{65,97},{97,1},{2,34}... | collective-permute-start | bytes 368648 | tf_op jit(solution)/shard_map/ppermute | solution.py:22
  10.9 10.3 %collective-permute-start.1 = (bf16[96,640]{1,0:T(8,128)(2,1)S(1)}, bf16[96,640]{1,0:T(8,128)(2,1)S(1)}, u32[]{:S(2)}, u32[]{:S(2)}) collective-permute-start(bf16[96,640]{1,0:T(8,128)(2,1)S(1)} %fusion.15), channel_id=1, source_target_pairs={{0,96},{32,0},{64,32},{96,64},{1,97},{33,1},{65,33},{97,65},{2,98}... | collective-permute-start | bytes 368648 | tf_op jit(solution)/shard_map/ppermute | solution.py:22
  13.3 8.0 %collective-permute-start.2 = (bf16[96,640]{1,0:T(8,128)(2,1)S(1)}, bf16[96,640]{1,0:T(8,128)(2,1)S(1)}, u32[]{:S(2)}, u32[]{:S(2)}) collective-permute-start(bf16[96,640]{1,0:T(8,128)(2,1)S(1)} %get-tuple-element.32), channel_id=1, source_target_pairs={{0,8},{8,16},{16,24},{24,0},{1,9},{9,17},{17,25},{25,1},{2,10},{10... | collective-permute-start | bytes 368648 | tf_op jit(solution)/shard_map/ppermute | solution.py:22
  15.1 6.2 %collective-permute-start.3 = (bf16[96,640]{1,0:T(8,128)(2,1)S(1)}, bf16[96,640]{1,0:T(8,128)(2,1)S(1)}, u32[]{:S(2)}, u32[]{:S(2)}) collective-permute-start(bf16[96,640]{1,0:T(8,128)(2,1)S(1)} %get-tuple-element.32), channel_id=1, source_target_pairs={{0,24},{8,0},{16,8},{24,16},{1,25},{9,1},{17,9},{25,17},{2,26},{10... | collective-permute-start | bytes 368648 | tf_op jit(solution)/shard_map/ppermute | solution.py:22
  19.9 10.6 %collective-permute-start.6 = (bf16[64,3072]{1,0:T(8,128)(2,1)S(1)}, bf16[64,3072]{1,0:T(8,128)(2,1)}, u32[]{:S(2)}, u32[]{:S(2)}) collective-permute-start(bf16[64,3072]{1,0:T(8,128)(2,1)S(1)} %reshape.234), channel_id=1, source_target_pairs={{0,2},{2,4},{4,6},{6,0},{1,3},{3,5},{5,7},{7,1},{8,10},{10,12},{12... | collective-permute-start | bytes 1179656 | tf_op jit(solution)/shard_map/ppermute | solution.py:22
  21.3 5.5 %collective-permute-start.4 = (bf16[96,640]{1,0:T(8,128)(2,1)S(1)}, bf16[96,640]{1,0:T(8,128)(2,1)S(1)}, u32[]{:S(2)}, u32[]{:S(2)}) collective-permute-start(bf16[96,640]{1,0:T(8,128)(2,1)S(1)} %fusion.15), channel_id=1, source_target_pairs={{0,64},{32,96},{64,0},{96,32},{1,65},{33,97},{65,1},{97,33},{2,66}... | collective-permute-start | bytes 368648 | tf_op jit(solution)/shard_map/ppermute | solution.py:22
  22.9 12.9 %collective-permute-start.8 = (bf16[64,3072]{1,0:T(8,128)(2,1)S(1)}, bf16[64,3072]{1,0:T(8,128)(2,1)}, u32[]{:S(2)}, u32[]{:S(2)}) collective-permute-start(bf16[64,3072]{1,0:T(8,128)(2,1)S(1)} %reshape.234), channel_id=1, source_target_pairs={{0,6},{2,0},{4,2},{6,4},{1,7},{3,1},{5,3},{7,5},{8,14},{10,8},{12,... | collective-permute-start | bytes 1179656 | tf_op jit(solution)/shard_map/ppermute | solution.py:22
  24.5 5.7 %collective-permute-start.5 = (bf16[96,640]{1,0:T(8,128)(2,1)S(1)}, bf16[96,640]{1,0:T(8,128)(2,1)S(1)}, u32[]{:S(2)}, u32[]{:S(2)}) collective-permute-start(bf16[96,640]{1,0:T(8,128)(2,1)S(1)} %get-tuple-element.32), channel_id=1, source_target_pairs={{0,16},{8,24},{16,0},{24,8},{1,17},{9,25},{17,1},{25,9},{2,18},{10... | collective-permute-start | bytes 368648 | tf_op jit(solution)/shard_map/ppermute | solution.py:22
  30.5 12.8 %collective-permute-start.10 = (bf16[4,96,640]{2,1,0:T(8,128)(2,1)S(1)}, bf16[4,96,640]{2,1,0:T(8,128)(2,1)S(1)}, u32[]{:S(2)}, u32[]{:S(2)}) collective-permute-start(bf16[4,96,640]{2,1,0:T(8,128)(2,1)S(1)} %pad_maximum_fusion.1.refs_0_), channel_id=1, source_target_pairs={{0,8},{8,16},{16,24},{24,0},{1,9},{9,17},{17,25},{25,1},{2,10},{10... | collective-permute-start | bytes 1474568 | tf_op jit(solution)/shard_map/ppermute | solution.py:22
  31.1 12.3 %collective-permute-start.11 = (bf16[4,96,640]{2,1,0:T(8,128)(2,1)S(1)}, bf16[4,96,640]{2,1,0:T(8,128)(2,1)S(1)}, u32[]{:S(2)}, u32[]{:S(2)}) collective-permute-start(bf16[4,96,640]{2,1,0:T(8,128)(2,1)S(1)} %pad_maximum_fusion.1.refs_0_), channel_id=1, source_target_pairs={{0,24},{8,0},{16,8},{24,16},{1,25},{9,1},{17,9},{25,17},{2,26},{10... | collective-permute-start | bytes 1474568 | tf_op jit(solution)/shard_map/ppermute | solution.py:22
  33.2 10.2 %collective-permute-start.12 = (bf16[4,96,640]{2,1,0:T(8,128)(2,1)S(1)}, bf16[4,96,640]{2,1,0:T(8,128)(2,1)S(1)}, u32[]{:S(2)}, u32[]{:S(2)}) collective-permute-start(bf16[4,96,640]{2,1,0:T(8,128)(2,1)S(1)} %pad_maximum_fusion.2.refs_5_), channel_id=1, source_target_pairs={{0,32},{32,64},{64,96},{96,0},{1,33},{33,65},{65,97},{97,1},{2,34}... | collective-permute-start | bytes 1474568 | tf_op jit(solution)/shard_map/ppermute | solution.py:22
  33.9 9.5 %collective-permute-start.13 = (bf16[4,96,640]{2,1,0:T(8,128)(2,1)S(1)}, bf16[4,96,640]{2,1,0:T(8,128)(2,1)S(1)}, u32[]{:S(2)}, u32[]{:S(2)}) collective-permute-start(bf16[4,96,640]{2,1,0:T(8,128)(2,1)S(1)} %pad_maximum_fusion.2.refs_5_), channel_id=1, source_target_pairs={{0,96},{32,0},{64,32},{96,64},{1,97},{33,1},{65,33},{97,65},{2,98}... | collective-permute-start | bytes 1474568 | tf_op jit(solution)/shard_map/ppermute | solution.py:22
  35.9 8.2 %collective-permute-start.9 = (bf16[64,3072]{1,0:T(8,128)(2,1)S(1)}, bf16[64,3072]{1,0:T(8,128)(2,1)}, u32[]{:S(2)}, u32[]{:S(2)}) collective-permute-start(bf16[64,3072]{1,0:T(8,128)(2,1)S(1)} %reshape.234), channel_id=1, source_target_pairs={{0,4},{2,6},{4,0},{6,2},{1,5},{3,7},{5,1},{7,3},{8,12},{10,14},{12... | collective-permute-start | bytes 1179656 | tf_op jit(solution)/shard_map/ppermute | solution.py:22
  45.8 22.9 %collective-permute-start.14 = (bf16[4,64,3072]{2,1,0:T(8,128)(2,1)S(1)}, bf16[4,64,3072]{2,1,0:T(8,128)(2,1)S(1)}, u32[]{:S(2)}, u32[]{:S(2)}) collective-permute-start(bf16[4,64,3072]{2,1,0:T(8,128)(2,1)S(1)} %pad_maximum_fusion.xo_ref), channel_id=1, source_target_pairs={{0,1},{1,0},{2,3},{3,2},{4,5},{5,4},{6,7},{7,6},{8,9},{9,8},{10,11... | collective-permute-start | bytes 4718600 | tf_op jit(solution)/shard_map/ppermute | solution.py:26
  56.9 8.4 %collective-permute-start.15 = (bf16[2,96,640]{2,1,0:T(8,128)(2,1)S(1)}, bf16[2,96,640]{2,1,0:T(8,128)(2,1)S(1)}, u32[]{:S(2)}, u32[]{:S(2)}) collective-permute-start(bf16[2,96,640]{2,1,0:T(8,128)(2,1)S(1)} %slice.85), channel_id=1, source_target_pairs={{0,8},{8,16},{16,24},{24,0},{1,9},{9,17},{17,25},{25,1},{2,10},{10... | collective-permute-start | bytes 737288 | tf_op jit(solution)/shard_map/ppermute | solution.py:22
  57.0 8.3 %collective-permute-start.16 = (bf16[2,96,640]{2,1,0:T(8,128)(2,1)S(1)}, bf16[2,96,640]{2,1,0:T(8,128)(2,1)S(1)}, u32[]{:S(2)}, u32[]{:S(2)}) collective-permute-start(bf16[2,96,640]{2,1,0:T(8,128)(2,1)S(1)} %slice.86), channel_id=1, source_target_pairs={{0,24},{8,0},{16,8},{24,16},{1,25},{9,1},{17,9},{25,17},{2,26},{10... | collective-permute-start | bytes 737288 | tf_op jit(solution)/shard_map/ppermute | solution.py:22
  59.7 8.9 %collective-permute-start.17 = (bf16[2,96,640]{2,1,0:T(8,128)(2,1)S(1)}, bf16[2,96,640]{2,1,0:T(8,128)(2,1)S(1)}, u32[]{:S(2)}, u32[]{:S(2)}) collective-permute-start(bf16[2,96,640]{2,1,0:T(8,128)(2,1)S(1)} %slice.87), channel_id=1, source_target_pairs={{0,32},{32,64},{64,96},{96,0},{1,33},{33,65},{65,97},{97,1},{2,34}... | collective-permute-start | bytes 737288 | tf_op jit(solution)/shard_map/ppermute | solution.py:22
  59.9 8.8 %collective-permute-start.18 = (bf16[2,96,640]{2,1,0:T(8,128)(2,1)S(1)}, bf16[2,96,640]{2,1,0:T(8,128)(2,1)S(1)}, u32[]{:S(2)}, u32[]{:S(2)}) collective-permute-start(bf16[2,96,640]{2,1,0:T(8,128)(2,1)S(1)} %slice.88), channel_id=1, source_target_pairs={{0,96},{32,0},{64,32},{96,64},{1,97},{33,1},{65,33},{97,65},{2,98}... | collective-permute-start | bytes 737288 | tf_op jit(solution)/shard_map/ppermute | solution.py:22
  79.2 4.5 %collective-permute-start.20 = (bf16[4,64,2880]{2,1,0:T(8,128)(2,1)S(1)}, bf16[4,64,2880]{2,1,0:T(8,128)(2,1)S(1)}, u32[]{:S(2)}, u32[]{:S(2)}) collective-permute-start(bf16[4,64,2880]{2,1,0:T(8,128)(2,1)S(1)} %other.1), channel_id=1, source_target_pairs={{0,1},{1,0},{2,3},{3,2},{4,5},{5,4},{6,7},{7,6},{8,9},{9,8},{10,11... | collective-permute-start | bytes 4423688 | tf_op jit(solution)/shard_map/ppermute | solution.py:26
  85.3 6.0 %collective-permute-start.23 = (bf16[32,2880]{1,0:T(8,128)(2,1)S(1)}, bf16[32,2880]{1,0:T(8,128)(2,1)S(1)}, u32[]{:S(2)}, u32[]{:S(2)}) collective-permute-start(bf16[32,2880]{1,0:T(8,128)(2,1)S(1)} %get-tuple-element.55), channel_id=1, source_target_pairs={{0,6},{2,0},{4,2},{6,4},{1,7},{3,1},{5,3},{7,5},{8,14},{10,8},{12,... | collective-permute-start | bytes 552968 | tf_op jit(solution)/shard_map/ppermute | solution.py:22
  86.0 7.2 %collective-permute-start.21 = (bf16[32,2880]{1,0:T(8,128)(2,1)S(1)}, bf16[32,2880]{1,0:T(8,128)(2,1)S(1)}, u32[]{:S(2)}, u32[]{:S(2)}) collective-permute-start(bf16[32,2880]{1,0:T(8,128)(2,1)S(1)} %get-tuple-element.53), channel_id=1, source_target_pairs={{0,2},{2,4},{4,6},{6,0},{1,3},{3,5},{5,7},{7,1},{8,10},{10,12},{12... | collective-permute-start | bytes 552968 | tf_op jit(solution)/shard_map/ppermute | solution.py:22
  91.4 9.1 %collective-permute-start.24 = (bf16[64,2880]{1,0:T(8,128)(2,1)S(1)}, bf16[64,2880]{1,0:T(8,128)(2,1)S(1)}, u32[]{:S(2)}, u32[]{:S(2)}) collective-permute-start(bf16[64,2880]{1,0:T(8,128)(2,1)S(1)} %pad_maximum_fusion.4), channel_id=1, source_target_pairs={{0,6},{2,0},{4,2},{6,4},{1,7},{3,1},{5,3},{7,5},{8,14},{10,8},{12,... | collective-permute-start | bytes 1105928 | tf_op jit(solution)/shard_map/ppermute | solution.py:22
  93.3 10.1 %collective-permute-start.22 = (bf16[64,2880]{1,0:T(8,128)(2,1)S(1)}, bf16[64,2880]{1,0:T(8,128)(2,1)S(1)}, u32[]{:S(2)}, u32[]{:S(2)}) collective-permute-start(bf16[64,2880]{1,0:T(8,128)(2,1)S(1)} %pad_maximum_fusion.3), channel_id=1, source_target_pairs={{0,2},{2,4},{4,6},{6,0},{1,3},{3,5},{5,7},{7,1},{8,10},{10,12},{12... | collective-permute-start | bytes 1105928 | tf_op jit(solution)/shard_map/ppermute | solution.py:22
  (13 other events, 83.7 us)
Sparse Core Ops, SparseCore 0:
  10.2 51.2 all-gather.2

commit v3 on v2

--- a/solution.py
+++ b/solution.py
@@ -298,7 +298,9 @@
     a_near, b_near = near(a, "x"), near(b, "z")
     spread = jnp.pad(normed.reshape(rows, 16, shard), ((0, 0), (0, 0), (0, 2 * depth - shard)))
     spread = spread.reshape(rows, 32 * depth)
-    x_fore = shifted(spread, "y", 1)
+    mine = jnp.concatenate([expert_ids.astype(F32), route_weights], axis=1)
+    theirs = swapped(mine)
+    x_fore = shifted(after(spread, theirs), "y", 1)
     a_far = shifted(after(a, *a_near, *b_near), "x", 2)
     b_far = shifted(after(b, *a_near, *b_near), "z", 2)
     x_back = shifted(after(spread, *a_near, *b_near), "y", -1)
@@ -312,8 +314,6 @@
     a_near, b_near = (a_fore, a_back), (b_fore, b_back)
     x_own = jnp.stack(x_parts)
     x_other = swapped(x_own)
-    mine = jnp.concatenate([expert_ids.astype(F32), route_weights], axis=1)
-    theirs = swapped(after(mine, a_stack, b_stack))
     a_parts = (a_stack, *a_near, *passed_on(a_near, "z"))
     b_parts = (b_stack, *b_near, *passed_on(b_near, "x"))
 

time: 238 us -> 243 us (1.021)
  waiting for transfers between devices: 36.2 us -> 41.5 us
    ppermute x21, waiting for transfers between devices: 27.1 us -> 35.4 us  [shifted(): lax.ppermute(block, axis, [(i, (i + distance) % 4) for i in range(4)])]
    ppermute x5, waiting for transfers between devices: 8.34 us -> 5.48 us  [swapped(): return lax.ppermute(block, 'c', [(0, 1), (1, 0)])]
  transfers between devices with their start and end apart: 28 -> 28, of which waited for: 13 -> 15; matrix products, arithmetic and copies ran while one was open for 4% -> 4% of each run, Pallas kernels for 2% -> 2%
where the time goes in v3:
time: 243 us
  blocking collectives  91.9 us (38%)
  starting transfers between devices  46.5 us (19%)
  waiting for transfers between devices  41.5 us (17%)
  Pallas kernels  35.6 us (15%)
  between operations  14.4 us (6%)
  other arithmetic  8.51 us (4%)
  local copies, waits for them, and re-layouts  3.9 us (2%)
    all_to_all x2, blocking collectives, on_device(): lax.all_to_all(array.reshape(64, 8, width), ('x', 'z', 'y'), split_axis=0...  91.9 us
    ppermute x21, waiting for transfers between devices, shifted(): lax.ppermute(block, axis, [(i, (i + distance) % 4) for i in range(4)])  35.4 us
    ppermute x21, starting transfers between devices, shifted(): lax.ppermute(block, axis, [(i, (i + distance) % 4) for i in range(4)])  30.1 us
    pallas_call x1, Pallas kernels, expert_ffn(): pl.pallas_call(functools.partial(expert_kernel, steps, width), grid=(step...  23.6 us
    ppermute x5, starting transfers between devices, swapped(): return lax.ppermute(block, 'c', [(0, 1), (1, 0)])  15.1 us
    ppermute x5, waiting for transfers between devices, swapped(): return lax.ppermute(block, 'c', [(0, 1), (1, 0)])  5.48 us
  transfers between devices with their start and end apart: 28, of which 15 were waited for; matrix products, arithmetic and copies ran while one was open for 4% of the time, Pallas kernels for 2%

profile of v3, /device:TPU:1, one launch (start us, length us, event | category | flops | bytes accessed | tf_op | source)
XLA Modules:
  0.0 242.7 jit_solution(827515670026741404)
XLA Ops:
  8.8 2.1 collective-permute-start.2
  15.1 2.2 collective-permute-start.5
  28.8 2.6 %collective-permute-done.7 = bf16[96,640]{1,0:T(8,128)(2,1)S(1)} collective-permute-done((bf16[96,640]{1,0:T(8,128)(2,1)S(1)}, bf16[96,640]{1,0:T(8,128)(2,1)S(1)}, u32[]{:S(2)}, u32[]{:S(2)}) %collective-permute-start.7) | collective-permute-done | bytes 122912 | tf_op jit(solution)/shard_map/ppermute | solution.py:22
  33.0 2.0 collective-permute-done.1
  35.0 2.7 %collective-permute-start.11 = (bf16[4,96,640]{2,1,0:T(8,128)(2,1)S(1)}, bf16[4,96,640]{2,1,0:T(8,128)(2,1)S(1)}, u32[]{:S(2)}, u32[]{:S(2)}) collective-permute-start(bf16[4,96,640]{2,1,0:T(8,128)(2,1)S(1)} %pad_maximum_fusion.1.refs_0_), channel_id=1, source_target_pairs={{0,24},{8,0},{16,8},{24,16},{1,25},{9,1},{17,9},{25,17},{2,26},{10... | collective-permute-start | bytes 1474568 | tf_op jit(solution)/shard_map/ppermute | solution.py:22
  37.7 2.7 %collective-permute-start.13 = (bf16[4,96,640]{2,1,0:T(8,128)(2,1)S(1)}, bf16[4,96,640]{2,1,0:T(8,128)(2,1)S(1)}, u32[]{:S(2)}, u32[]{:S(2)}) collective-permute-start(bf16[4,96,640]{2,1,0:T(8,128)(2,1)S(1)} %pad_maximum_fusion.2.refs_5_), channel_id=1, source_target_pairs={{0,96},{32,0},{64,32},{96,64},{1,97},{33,1},{65,33},{97,65},{2,98}... | collective-permute-start | bytes 1474568 | tf_op jit(solution)/shard_map/ppermute | solution.py:22
  43.7 4.7 %collective-permute-done.10.refs_1_ = bf16[4,96,640]{2,1,0:T(8,128)(2,1)S(1)} collective-permute-done((bf16[4,96,640]{2,1,0:T(8,128)(2,1)S(1)}, bf16[4,96,640]{2,1,0:T(8,128)(2,1)S(1)}, u32[]{:S(2)}, u32[]{:S(2)}) %collective-permute-start.10) | collective-permute-done | bytes 491552 | tf_op jit(solution)/shard_map/ppermute | solution.py:22
  49.3 3.0 %collective-permute-done.12.refs_6_ = bf16[4,96,640]{2,1,0:T(8,128)(2,1)S(1)} collective-permute-done((bf16[4,96,640]{2,1,0:T(8,128)(2,1)S(1)}, bf16[4,96,640]{2,1,0:T(8,128)(2,1)S(1)}, u32[]{:S(2)}, u32[]{:S(2)}) %collective-permute-start.12) | collective-permute-done | bytes 491552 | tf_op jit(solution)/shard_map/ppermute | solution.py:22
  55.0 6.8 %collective-permute-start.14 = (bf16[4,64,3072]{2,1,0:T(8,128)(2,1)S(1)}, bf16[4,64,3072]{2,1,0:T(8,128)(2,1)S(1)}, u32[]{:S(2)}, u32[]{:S(2)}) collective-permute-start(bf16[4,64,3072]{2,1,0:T(8,128)(2,1)S(1)} %pad_maximum_fusion.xo_ref), channel_id=1, source_target_pairs={{0,1},{1,0},{2,3},{3,2},{4,5},{5,4},{6,7},{7,6},{8,9},{9,8},{10,11... | collective-permute-start | bytes 4718600 | tf_op jit(solution)/shard_map/ppermute | solution.py:26
  63.0 2.7 %collective-permute-start.16 = (bf16[2,96,640]{2,1,0:T(8,128)(2,1)S(1)}, bf16[2,96,640]{2,1,0:T(8,128)(2,1)S(1)}, u32[]{:S(2)}, u32[]{:S(2)}) collective-permute-start(bf16[2,96,640]{2,1,0:T(8,128)(2,1)S(1)} %slice.86), channel_id=1, source_target_pairs={{0,24},{8,0},{16,8},{24,16},{1,25},{9,1},{17,9},{25,17},{2,26},{10... | collective-permute-start | bytes 737288 | tf_op jit(solution)/shard_map/ppermute | solution.py:22
  65.8 3.6 %collective-permute-start.18 = (bf16[2,96,640]{2,1,0:T(8,128)(2,1)S(1)}, bf16[2,96,640]{2,1,0:T(8,128)(2,1)S(1)}, u32[]{:S(2)}, u32[]{:S(2)}) collective-permute-start(bf16[2,96,640]{2,1,0:T(8,128)(2,1)S(1)} %slice.88), channel_id=1, source_target_pairs={{0,96},{32,0},{64,32},{96,64},{1,97},{33,1},{65,33},{97,65},{2,98}... | collective-permute-start | bytes 737288 | tf_op jit(solution)/shard_map/ppermute | solution.py:22
  69.7 2.0 collective-permute-done.15.refs_3_
  71.7 3.3 %collective-permute-done.17.refs_8_ = bf16[2,96,640]{2,1,0:T(8,128)(2,1)S(1)} collective-permute-done((bf16[2,96,640]{2,1,0:T(8,128)(2,1)S(1)}, bf16[2,96,640]{2,1,0:T(8,128)(2,1)S(1)}, u32[]{:S(2)}, u32[]{:S(2)}) %collective-permute-start.17) | collective-permute-done | bytes 245792 | tf_op jit(solution)/shard_map/ppermute | solution.py:22
  75.0 3.8 %projection.1 = (bf16[512,512]{1,0:T(8,128)(2,1)S(1)}, bf16[512,128]{1,0:T(8,128)(2,1)S(1)}) custom-call(s32[4]{0:T(128)S(1)} %pad_add_fusion.at_ref, f32[512,128]{1,0:T(8,128)S(1)} %get-tuple-element.83.cos_ref, f32[512,128]{1,0:T(8,128)S(1)} %get-tuple-element.84.sin_ref, bf16[4,64,3072]{2,1,0:T(8,128)(2,1)S(1)} %pad_maximum_fusion.xo_ref, ...), custom_call_target="tpu_custom_call" | custom-call | flops 1887436800 | bytes 12000000 | tf_op jit(solution)/shard_map/projection/pallas_call | solution.py:333
  80.2 1.8 later.1.later_ref
  86.7 2.9 %collective-permute-done.20.got_ref = bf16[4,64,2880]{2,1,0:T(8,128)(2,1)S(1)} collective-permute-done((bf16[4,64,2880]{2,1,0:T(8,128)(2,1)S(1)}, bf16[4,64,2880]{2,1,0:T(8,128)(2,1)S(1)}, u32[]{:S(2)}, u32[]{:S(2)}) %collective-permute-start.20) | collective-permute-done | bytes 1474592 | tf_op jit(solution)/shard_map/ppermute | solution.py:26
  92.9 4.3 %collective-permute-done.23 = bf16[32,2880]{1,0:T(8,128)(2,1)S(1)} collective-permute-done((bf16[32,2880]{1,0:T(8,128)(2,1)S(1)}, bf16[32,2880]{1,0:T(8,128)(2,1)S(1)}, u32[]{:S(2)}, u32[]{:S(2)}) %collective-permute-start.23) | collective-permute-done | bytes 184352 | tf_op jit(solution)/shard_map/ppermute | solution.py:22
  99.0 7.4 %collective-permute-done.24 = bf16[64,2880]{1,0:T(8,128)(2,1)S(1)} collective-permute-done((bf16[64,2880]{1,0:T(8,128)(2,1)S(1)}, bf16[64,2880]{1,0:T(8,128)(2,1)S(1)}, u32[]{:S(2)}, u32[]{:S(2)}) %collective-permute-start.24) | collective-permute-done | bytes 368672 | tf_op jit(solution)/shard_map/ppermute | solution.py:22
  106.4 2.4 %collective-permute-done.22 = bf16[64,2880]{1,0:T(8,128)(2,1)S(1)} collective-permute-done((bf16[64,2880]{1,0:T(8,128)(2,1)S(1)}, bf16[64,2880]{1,0:T(8,128)(2,1)S(1)}, u32[]{:S(2)}, u32[]{:S(2)}) %collective-permute-start.22) | collective-permute-done | bytes 368672 | tf_op jit(solution)/shard_map/ppermute | solution.py:22
  109.3 2.5 %collective-permute-start.25 = (bf16[64,2880]{1,0:T(8,128)(2,1)S(1)}, bf16[64,2880]{1,0:T(8,128)(2,1)S(1)}, u32[]{:S(2)}, u32[]{:S(2)}) collective-permute-start(bf16[64,2880]{1,0:T(8,128)(2,1)S(1)} %fusion.2.own_ref), channel_id=1, source_target_pairs={{0,1},{1,0},{2,3},{3,2},{4,5},{5,4},{6,7},{7,6},{8,9},{9,8},{10,11... | collective-permute-start | bytes 1105928 | tf_op jit(solution)/shard_map/ppermute | solution.py:26
  114.1 47.8 %all_to_all.10 = bf16[64,8,2880]{2,1,0:T(8,128)(2,1)} all-to-all(bf16[64,8,2880]{2,1,0:T(8,128)(2,1)S(1)} %bitcast.51), channel_id=1, replica_groups=mesh['x'=4,'z'=4,'y'=4,'c'=2] {'x','z','y'}, dimensions={0} | all-to-all | bytes 5898240 | tf_op jit(solution)/shard_map/all_to_all | solution.py:403
  161.9 23.6 %experts.1 = bf16[512,2880]{1,0:T(8,128)(2,1)} custom-call(bf16[512,2880]{1,0:T(8,128)(2,1)} %bitcast.54, bf16[1,2880,2880]{2,1,0:T(8,128)(2,1)} %gu_ref.1, bf16[1,1440,2880]{2,1,0:T(8,128)(2,1)} %down_ref.1), custom_call_target="tpu_custom_call" | custom-call | flops 12740198400 | bytes 31000000 | tf_op jit(solution)/shard_map/experts/pallas_call | solution.py:241
  185.5 44.1 %all_to_all.11 = bf16[64,8,2880]{2,1,0:T(8,128)(2,1)S(1)} all-to-all(bf16[64,8,2880]{2,1,0:T(8,128)(2,1)} %bitcast.55), channel_id=1, replica_groups=mesh['x'=4,'z'=4,'y'=4,'c'=2] {'x','z','y'}, dimensions={0} | all-to-all | bytes 5898240 | tf_op jit(solution)/shard_map/all_to_all | solution.py:403
  230.6 3.1 %collective-permute-start.26 = (bf16[64,2880]{1,0:T(8,128)(2,1)S(1)}, bf16[64,2880]{1,0:T(8,128)(2,1)S(1)}, u32[]{:S(2)}, u32[]{:S(2)}) collective-permute-start(bf16[64,2880]{1,0:T(8,128)(2,1)S(1)} %get-tuple-element.59), channel_id=1, source_target_pairs={{0,1},{1,0},{2,3},{3,2},{4,5},{5,4},{6,7},{7,6},{8,9},{9,8},{10,11... | collective-permute-start | bytes 1105928 | tf_op jit(solution)/shard_map/ppermute | solution.py:26
  (107 shorter events, 44.0 us)
Async XLA Ops:
  7.2 74.9 %all-gather.3.cloned.1.call-start = ((), (), s32[]{:S(2)}) async-start(), calls=%async_computation.2 | async-start | bytes 3203072 | tf_op jit(solution)/shard_map/all_gather | solution.py:291
  8.8 15.3 %collective-permute-start.2 = (bf16[96,640]{1,0:T(8,128)(2,1)S(1)}, bf16[96,640]{1,0:T(8,128)(2,1)S(1)}, u32[]{:S(2)}, u32[]{:S(2)}) collective-permute-start(bf16[96,640]{1,0:T(8,128)(2,1)S(1)} %fusion.15), channel_id=1, source_target_pairs={{0,32},{32,64},{64,96},{96,0},{1,33},{33,65},{65,97},{97,1},{2,34}... | collective-permute-start | bytes 368648 | tf_op jit(solution)/shard_map/ppermute | solution.py:22
  10.9 13.2 %collective-permute-start.3 = (bf16[96,640]{1,0:T(8,128)(2,1)S(1)}, bf16[96,640]{1,0:T(8,128)(2,1)S(1)}, u32[]{:S(2)}, u32[]{:S(2)}) collective-permute-start(bf16[96,640]{1,0:T(8,128)(2,1)S(1)} %fusion.15), channel_id=1, source_target_pairs={{0,96},{32,0},{64,32},{96,64},{1,97},{33,1},{65,33},{97,65},{2,98}... | collective-permute-start | bytes 368648 | tf_op jit(solution)/shard_map/ppermute | solution.py:22
  13.3 10.9 %collective-permute-start.4 = (bf16[96,640]{1,0:T(8,128)(2,1)S(1)}, bf16[96,640]{1,0:T(8,128)(2,1)S(1)}, u32[]{:S(2)}, u32[]{:S(2)}) collective-permute-start(bf16[96,640]{1,0:T(8,128)(2,1)S(1)} %get-tuple-element.35), channel_id=1, source_target_pairs={{0,8},{8,16},{16,24},{24,0},{1,9},{9,17},{17,25},{25,1},{2,10},{10... | collective-permute-start | bytes 368648 | tf_op jit(solution)/shard_map/ppermute | solution.py:22
  15.1 9.0 %collective-permute-start.5 = (bf16[96,640]{1,0:T(8,128)(2,1)S(1)}, bf16[96,640]{1,0:T(8,128)(2,1)S(1)}, u32[]{:S(2)}, u32[]{:S(2)}) collective-permute-start(bf16[96,640]{1,0:T(8,128)(2,1)S(1)} %get-tuple-element.35), channel_id=1, source_target_pairs={{0,24},{8,0},{16,8},{24,16},{1,25},{9,1},{17,9},{25,17},{2,26},{10... | collective-permute-start | bytes 368648 | tf_op jit(solution)/shard_map/ppermute | solution.py:22
  22.8 12.3 %collective-permute-start.1 = (bf16[64,3072]{1,0:T(8,128)(2,1)S(1)}, bf16[64,3072]{1,0:T(8,128)(2,1)}, u32[]{:S(2)}, u32[]{:S(2)}) collective-permute-start(bf16[64,3072]{1,0:T(8,128)(2,1)S(1)} %reshape.234), channel_id=1, source_target_pairs={{0,2},{2,4},{4,6},{6,0},{1,3},{3,5},{5,7},{7,1},{8,10},{10,12},{12... | collective-permute-start | bytes 1179656 | tf_op jit(solution)/shard_map/ppermute | solution.py:22
  24.2 7.2 %collective-permute-start.7 = (bf16[96,640]{1,0:T(8,128)(2,1)S(1)}, bf16[96,640]{1,0:T(8,128)(2,1)S(1)}, u32[]{:S(2)}, u32[]{:S(2)}) collective-permute-start(bf16[96,640]{1,0:T(8,128)(2,1)S(1)} %fusion.15), channel_id=1, source_target_pairs={{0,64},{32,96},{64,0},{96,32},{1,65},{33,97},{65,1},{97,33},{2,66}... | collective-permute-start | bytes 368648 | tf_op jit(solution)/shard_map/ppermute | solution.py:22
  25.8 14.6 %collective-permute-start.6 = (bf16[64,3072]{1,0:T(8,128)(2,1)S(1)}, bf16[64,3072]{1,0:T(8,128)(2,1)S(1)}, u32[]{:S(2)}, u32[]{:S(2)}) collective-permute-start(bf16[64,3072]{1,0:T(8,128)(2,1)S(1)} %reshape.234), channel_id=1, source_target_pairs={{0,6},{2,0},{4,2},{6,4},{1,7},{3,1},{5,3},{7,5},{8,14},{10,8},{12,... | collective-permute-start | bytes 1179656 | tf_op jit(solution)/shard_map/ppermute | solution.py:22
  27.3 5.7 %collective-permute-start.8 = (bf16[96,640]{1,0:T(8,128)(2,1)S(1)}, bf16[96,640]{1,0:T(8,128)(2,1)S(1)}, u32[]{:S(2)}, u32[]{:S(2)}) collective-permute-start(bf16[96,640]{1,0:T(8,128)(2,1)S(1)} %get-tuple-element.35), channel_id=1, source_target_pairs={{0,16},{8,24},{16,0},{24,8},{1,17},{9,25},{17,1},{25,9},{2,18},{10... | collective-permute-start | bytes 368648 | tf_op jit(solution)/shard_map/ppermute | solution.py:22
  35.0 13.4 %collective-permute-start.10 = (bf16[4,96,640]{2,1,0:T(8,128)(2,1)S(1)}, bf16[4,96,640]{2,1,0:T(8,128)(2,1)S(1)}, u32[]{:S(2)}, u32[]{:S(2)}) collective-permute-start(bf16[4,96,640]{2,1,0:T(8,128)(2,1)S(1)} %pad_maximum_fusion.1.refs_0_), channel_id=1, source_target_pairs={{0,8},{8,16},{16,24},{24,0},{1,9},{9,17},{17,25},{25,1},{2,10},{10... | collective-permute-start | bytes 1474568 | tf_op jit(solution)/shard_map/ppermute | solution.py:22
  35.0 14.3 %collective-permute-start.11 = (bf16[4,96,640]{2,1,0:T(8,128)(2,1)S(1)}, bf16[4,96,640]{2,1,0:T(8,128)(2,1)S(1)}, u32[]{:S(2)}, u32[]{:S(2)}) collective-permute-start(bf16[4,96,640]{2,1,0:T(8,128)(2,1)S(1)} %pad_maximum_fusion.1.refs_0_), channel_id=1, source_target_pairs={{0,24},{8,0},{16,8},{24,16},{1,25},{9,1},{17,9},{25,17},{2,26},{10... | collective-permute-start | bytes 1474568 | tf_op jit(solution)/shard_map/ppermute | solution.py:22
  37.7 14.6 %collective-permute-start.12 = (bf16[4,96,640]{2,1,0:T(8,128)(2,1)S(1)}, bf16[4,96,640]{2,1,0:T(8,128)(2,1)S(1)}, u32[]{:S(2)}, u32[]{:S(2)}) collective-permute-start(bf16[4,96,640]{2,1,0:T(8,128)(2,1)S(1)} %pad_maximum_fusion.2.refs_5_), channel_id=1, source_target_pairs={{0,32},{32,64},{64,96},{96,0},{1,33},{33,65},{65,97},{97,1},{2,34}... | collective-permute-start | bytes 1474568 | tf_op jit(solution)/shard_map/ppermute | solution.py:22
  37.7 15.8 %collective-permute-start.13 = (bf16[4,96,640]{2,1,0:T(8,128)(2,1)S(1)}, bf16[4,96,640]{2,1,0:T(8,128)(2,1)S(1)}, u32[]{:S(2)}, u32[]{:S(2)}) collective-permute-start(bf16[4,96,640]{2,1,0:T(8,128)(2,1)S(1)} %pad_maximum_fusion.2.refs_5_), channel_id=1, source_target_pairs={{0,96},{32,0},{64,32},{96,64},{1,97},{33,1},{65,33},{97,65},{2,98}... | collective-permute-start | bytes 1474568 | tf_op jit(solution)/shard_map/ppermute | solution.py:22
  41.2 12.4 %collective-permute-start.9 = (bf16[64,3072]{1,0:T(8,128)(2,1)S(1)}, bf16[64,3072]{1,0:T(8,128)(2,1)}, u32[]{:S(2)}, u32[]{:S(2)}) collective-permute-start(bf16[64,3072]{1,0:T(8,128)(2,1)S(1)} %reshape.234), channel_id=1, source_target_pairs={{0,4},{2,6},{4,0},{6,2},{1,5},{3,7},{5,1},{7,3},{8,12},{10,14},{12... | collective-permute-start | bytes 1179656 | tf_op jit(solution)/shard_map/ppermute | solution.py:22
  55.0 20.0 %collective-permute-start.14 = (bf16[4,64,3072]{2,1,0:T(8,128)(2,1)S(1)}, bf16[4,64,3072]{2,1,0:T(8,128)(2,1)S(1)}, u32[]{:S(2)}, u32[]{:S(2)}) collective-permute-start(bf16[4,64,3072]{2,1,0:T(8,128)(2,1)S(1)} %pad_maximum_fusion.xo_ref), channel_id=1, source_target_pairs={{0,1},{1,0},{2,3},{3,2},{4,5},{5,4},{6,7},{7,6},{8,9},{9,8},{10,11... | collective-permute-start | bytes 4718600 | tf_op jit(solution)/shard_map/ppermute | solution.py:26
  62.9 8.8 %collective-permute-start.15 = (bf16[2,96,640]{2,1,0:T(8,128)(2,1)S(1)}, bf16[2,96,640]{2,1,0:T(8,128)(2,1)S(1)}, u32[]{:S(2)}, u32[]{:S(2)}) collective-permute-start(bf16[2,96,640]{2,1,0:T(8,128)(2,1)S(1)} %slice.85), channel_id=1, source_target_pairs={{0,8},{8,16},{16,24},{24,0},{1,9},{9,17},{17,25},{25,1},{2,10},{10... | collective-permute-start | bytes 737288 | tf_op jit(solution)/shard_map/ppermute | solution.py:22
  63.0 8.7 %collective-permute-start.16 = (bf16[2,96,640]{2,1,0:T(8,128)(2,1)S(1)}, bf16[2,96,640]{2,1,0:T(8,128)(2,1)S(1)}, u32[]{:S(2)}, u32[]{:S(2)}) collective-permute-start(bf16[2,96,640]{2,1,0:T(8,128)(2,1)S(1)} %slice.86), channel_id=1, source_target_pairs={{0,24},{8,0},{16,8},{24,16},{1,25},{9,1},{17,9},{25,17},{2,26},{10... | collective-permute-start | bytes 737288 | tf_op jit(solution)/shard_map/ppermute | solution.py:22
  65.7 9.2 %collective-permute-start.17 = (bf16[2,96,640]{2,1,0:T(8,128)(2,1)S(1)}, bf16[2,96,640]{2,1,0:T(8,128)(2,1)S(1)}, u32[]{:S(2)}, u32[]{:S(2)}) collective-permute-start(bf16[2,96,640]{2,1,0:T(8,128)(2,1)S(1)} %slice.87), channel_id=1, source_target_pairs={{0,32},{32,64},{64,96},{96,0},{1,33},{33,65},{65,97},{97,1},{2,34}... | collective-permute-start | bytes 737288 | tf_op jit(solution)/shard_map/ppermute | solution.py:22
  65.8 9.1 %collective-permute-start.18 = (bf16[2,96,640]{2,1,0:T(8,128)(2,1)S(1)}, bf16[2,96,640]{2,1,0:T(8,128)(2,1)S(1)}, u32[]{:S(2)}, u32[]{:S(2)}) collective-permute-start(bf16[2,96,640]{2,1,0:T(8,128)(2,1)S(1)} %slice.88), channel_id=1, source_target_pairs={{0,96},{32,0},{64,32},{96,64},{1,97},{33,1},{65,33},{97,65},{2,98}... | collective-permute-start | bytes 737288 | tf_op jit(solution)/shard_map/ppermute | solution.py:22
  91.2 6.0 %collective-permute-start.23 = (bf16[32,2880]{1,0:T(8,128)(2,1)S(1)}, bf16[32,2880]{1,0:T(8,128)(2,1)S(1)}, u32[]{:S(2)}, u32[]{:S(2)}) collective-permute-start(bf16[32,2880]{1,0:T(8,128)(2,1)S(1)} %get-tuple-element.55), channel_id=1, source_target_pairs={{0,6},{2,0},{4,2},{6,4},{1,7},{3,1},{5,3},{7,5},{8,14},{10,8},{12,... | collective-permute-start | bytes 552968 | tf_op jit(solution)/shard_map/ppermute | solution.py:22
  91.5 7.2 %collective-permute-start.21 = (bf16[32,2880]{1,0:T(8,128)(2,1)S(1)}, bf16[32,2880]{1,0:T(8,128)(2,1)S(1)}, u32[]{:S(2)}, u32[]{:S(2)}) collective-permute-start(bf16[32,2880]{1,0:T(8,128)(2,1)S(1)} %get-tuple-element.53), channel_id=1, source_target_pairs={{0,2},{2,4},{4,6},{6,0},{1,3},{3,5},{5,7},{7,1},{8,10},{10,12},{12... | collective-permute-start | bytes 552968 | tf_op jit(solution)/shard_map/ppermute | solution.py:22
  97.3 9.1 %collective-permute-start.24 = (bf16[64,2880]{1,0:T(8,128)(2,1)S(1)}, bf16[64,2880]{1,0:T(8,128)(2,1)S(1)}, u32[]{:S(2)}, u32[]{:S(2)}) collective-permute-start(bf16[64,2880]{1,0:T(8,128)(2,1)S(1)} %pad_maximum_fusion.4), channel_id=1, source_target_pairs={{0,6},{2,0},{4,2},{6,4},{1,7},{3,1},{5,3},{7,5},{8,14},{10,8},{12,... | collective-permute-start | bytes 1105928 | tf_op jit(solution)/shard_map/ppermute | solution.py:22
  98.8 10.1 %collective-permute-start.22 = (bf16[64,2880]{1,0:T(8,128)(2,1)S(1)}, bf16[64,2880]{1,0:T(8,128)(2,1)S(1)}, u32[]{:S(2)}, u32[]{:S(2)}) collective-permute-start(bf16[64,2880]{1,0:T(8,128)(2,1)S(1)} %pad_maximum_fusion.3), channel_id=1, source_target_pairs={{0,2},{2,4},{4,6},{6,0},{1,3},{3,5},{5,7},{7,1},{8,10},{10,12},{12... | collective-permute-start | bytes 1105928 | tf_op jit(solution)/shard_map/ppermute | solution.py:22
  230.6 4.4 %collective-permute-start.26 = (bf16[64,2880]{1,0:T(8,128)(2,1)S(1)}, bf16[64,2880]{1,0:T(8,128)(2,1)S(1)}, u32[]{:S(2)}, u32[]{:S(2)}) collective-permute-start(bf16[64,2880]{1,0:T(8,128)(2,1)S(1)} %get-tuple-element.59), channel_id=1, source_target_pairs={{0,1},{1,0},{2,3},{3,2},{4,5},{5,4},{6,7},{7,6},{8,9},{9,8},{10,11... | collective-permute-start | bytes 1105928 | tf_op jit(solution)/shard_map/ppermute | solution.py:26
  (13 other events, 90.8 us)
Sparse Core Ops, SparseCore 0:
  10.2 54.2 all-gather.2
